TPU v7x, 32 devices: a whole 2x2x4 slice. The times are simulated.
32 devices in a mesh: seq: 16 (over z, x, core), dp: 2 (over y).
Axes of the slice: x: 2, y: 2, z: 4, core: 2. Of those that a mesh axis runs over, the one named last changes fastest.
Arguments:
- tokens: bfloat16 [2, 6272, 1024], P('dp', 'seq'), may hold values from -6 to 6
- clip_start: int32 [2, 32], P('dp', 'seq'), may hold values from 0 to 28, as said below
- frames: int32 [2, 32], P('dp', 'seq'), may hold values from 8 to 32, as said below
- positions: int32 [2, 3, 6272], P('dp', None, 'seq'), may hold values from 0 to 15, as said below
- first_gain: float32 [1024], replicated, may hold values from 0.5 to 1.5
- first_offset: float32 [1024], replicated, may hold values from -3 to 3
- triple_weight: bfloat16 [1024, 3072], replicated, may hold values from -0.1875 to 0.1875
- triple_bias: float32 [3072], replicated, may hold values from -0.75 to 0.75
- output_weight: bfloat16 [1024, 1024], replicated, may hold values from -3 to 3
- output_bias: float32 [1024], replicated, may hold values from -1.5 to 1.5
- second_gain: float32 [1024], replicated, may hold values from 0.5 to 1.5
- second_offset: float32 [1024], replicated, may hold values from -3 to 3
- expand_weight: bfloat16 [1024, 4096], replicated, may hold values from -0.1875 to 0.1875
- expand_bias: float32 [4096], replicated, may hold values from -3 to 3
- reduce_weight: bfloat16 [4096, 1024], replicated, may hold values from -0.09375 to 0.09375
- reduce_bias: float32 [1024], replicated, may hold values from -1.5 to 1.5
- cotangent: bfloat16 [2, 6272, 1024], P('dp', 'seq'), may hold values from -6 to 6
Outputs:
- result: bfloat16 [2, 6272, 1024], P('dp', 'seq')
- input_grad: float32 [2, 6272, 1024], P('dp', 'seq')
- grad_first_gain: float32 [1024], P(('seq', 'dp'))
- grad_first_offset: float32 [1024], P(('seq', 'dp'))
- grad_triple_weight: float32 [1024, 3072], P(('seq', 'dp'))
- grad_query_key_bias: float32 [2048], P(('seq', 'dp'))
- grad_value_bias: float32 [1024], P(('seq', 'dp'))
- grad_output_weight: float32 [1024, 1024], P(('seq', 'dp'))
- grad_output_bias: float32 [1024], P(('seq', 'dp'))
- grad_second_gain: float32 [1024], P(('seq', 'dp'))
- grad_second_offset: float32 [1024], P(('seq', 'dp'))
- grad_expand_weight: float32 [1024, 4096], P(('seq', 'dp'))
- grad_expand_bias: float32 [4096], P(('seq', 'dp'))
- grad_reduce_weight: float32 [4096, 1024], P(('seq', 'dp'))
- grad_reduce_bias: float32 [1024], P(('seq', 'dp'))
Inputs may be any that keep to these rules, and one draw needn't show every extreme that they name: `clip_start`: each group's 32 slabs are split into whole clips of 4, 8 or 16 slabs that begin at multiples of 4; every slab of a clip holds the clip's first slab, and every group has a clip of 16 slabs. `frames`: twice the number of slabs of the slab's clip. `positions`: row 0 is the token's slab minus its clip's first slab; rows 1 and 2 are the token's row and column in its 14 x 14 frame plus an offset of 0 to 2 that is one for each clip and direction.
All inputs are finite; a program needn't handle non-finite values.
Results may differ from a plain program's by a relative error of at most 0.023.
Values may be sent and summed in bfloat16 or wider, within the bound.
No kernel may reach another device: no remote copies, remote signals or barrier semaphores. Data moves between devices by JAX's collectives and lax.ppermute only.
A program may use at most 384 MiB of HBM per device.

v0:
```python
import jax
import jax.numpy as jnp
from jax import lax
from jax.sharding import PartitionSpec as P

HEAD_DIM = 64
CLIP_MIN = 4
CLIP_MAX = 16
REACH = 7


EPSILON = 1e-06
NEGATIVE = -1e30
SECTIONS = ((0, 10, 0), (20, 11, 10), (42, 11, 21))


def shifted(shard, axis, by):
    length = lax.axis_size(axis)
    pairs = [(i, i + by) for i in range(length) if 0 <= i + by < length]
    return lax.ppermute(shard, axis, pairs)


def layer_norm(inputs, norm_gain, norm_offset):
    centred = inputs - jnp.mean(inputs, axis=-1, keepdims=True)
    spread = jnp.mean(centred * centred, axis=-1, keepdims=True)
    return centred * lax.rsqrt(spread + EPSILON) * norm_gain + norm_offset


def rotary_tables(positions):
    angles = []
    for section, (begin_at, pair_count, first_pair) in enumerate(SECTIONS):
        frequency = jnp.power(10000.0, -jnp.arange(pair_count, dtype=jnp.float32) / pair_count)
        angles.append(positions[..., section, :].astype(jnp.float32)[..., None] * frequency)
    joined = jnp.concatenate(angles, axis=-1)
    return (jnp.cos(joined), jnp.sin(joined))


def rotate(inputs, cos_table, sin_table):
    pieces = []
    for begin_at, pair_count, first_pair in SECTIONS:
        low_half = inputs[..., begin_at : begin_at + pair_count]
        high_half = inputs[..., begin_at + pair_count : begin_at + 2 * pair_count]
        cos_part = cos_table[..., None, first_pair : first_pair + pair_count]
        sin_part = sin_table[..., None, first_pair : first_pair + pair_count]
        pieces.append(low_half * cos_part - high_half * sin_part)
        pieces.append(high_half * cos_part + low_half * sin_part)
    return jnp.concatenate(pieces, axis=-1)


def slab_bounds(clip_start, frames, first_slab, group_slabs):
    slab_index = first_slab + jnp.arange(clip_start.shape[-1], dtype=jnp.int32)
    unit_base = slab_index // CLIP_MIN * CLIP_MIN
    lower_slab = jnp.maximum(
        jnp.maximum(jnp.minimum(clip_start, slab_index), unit_base - (CLIP_MAX - CLIP_MIN)), 0
    )
    upper_slab = jnp.minimum(
        jnp.minimum(jnp.maximum(clip_start + frames // 2, slab_index + 1), unit_base + CLIP_MAX),
        group_slabs,
    )
    return (lower_slab, upper_slab, slab_index)


def score_block(queries, key_rows):
    return jnp.einsum("qhd,khd->hqk", queries, key_rows, preferred_element_type=jnp.float32) * 0.125


def contract_rows(left_side, right_side):
    return lax.dot_general(
        left_side, right_side, (((0,), (0,)), ((), ())), preferred_element_type=jnp.float32
    )


def contract_cols(left_side, right_side):
    return lax.dot_general(
        left_side, right_side, (((1,), (1,)), ((), ())), preferred_element_type=jnp.float32
    )


def gelu_exact(inputs):
    return jax.nn.gelu(inputs, approximate=False)


def keep_state(state_in):
    return state_in


def per_device(
    tokens,
    clip_start,
    frames,
    positions,
    first_gain,
    first_offset,
    triple_weight,
    triple_bias,
    output_weight,
    output_bias,
    second_gain,
    second_offset,
    expand_weight,
    expand_bias,
    reduce_weight,
    reduce_bias,
    cotangent,
):
    inputs = tokens[0].astype(jnp.float32)
    row_count, model_width = inputs.shape
    slab_count = clip_start.shape[1]
    per_slab = row_count // slab_count
    head_count = model_width // HEAD_DIM
    group_slabs = lax.axis_size("seq") * slab_count
    lower_slab, upper_slab, slab_index = slab_bounds(
        clip_start[0], frames[0], lax.axis_index("seq") * slab_count, group_slabs
    )
    query_lower = jnp.repeat(lower_slab, per_slab)
    query_upper = jnp.repeat(upper_slab, per_slab)
    token_slab = jnp.repeat(slab_index, per_slab)
    cos_table, sin_table = rotary_tables(positions[0])
    normed = layer_norm(inputs, first_gain, first_offset)
    normed_low = normed.astype(jnp.bfloat16)
    triple = jnp.dot(normed_low, triple_weight, preferred_element_type=jnp.float32) + triple_bias
    shaped = triple.reshape(row_count, 3, head_count, HEAD_DIM)
    query_raw = shaped[:, 0]
    key_raw = shaped[:, 1]
    query_rot = rotate(query_raw, cos_table, sin_table).astype(jnp.bfloat16)
    key_rot = rotate(key_raw, cos_table, sin_table).astype(jnp.bfloat16)
    value_low = shaped[:, 2].astype(jnp.bfloat16)
    packed = jnp.concatenate(
        [key_rot.reshape(row_count, model_width), value_low.reshape(row_count, model_width)], axis=1
    )
    offsets = [0]
    for distance in range(1, REACH + 1):
        offsets = offsets + [distance, -distance]
    received = [packed]
    for offset_now in offsets[1:]:
        received.append(shifted(packed, "seq", offset_now))
    stacked = jnp.stack(received).reshape(len(offsets), row_count, 2, head_count, HEAD_DIM)
    shift_table = jnp.array(offsets, dtype=jnp.int32)

    def piece_mask(offset_now):
        key_slab = token_slab - offset_now * slab_count
        allowed = (query_lower[:, None] <= key_slab[None, :]) & (
            key_slab[None, :] < query_upper[:, None]
        )
        return (allowed, jnp.any(allowed))

    def stats_step(running, scan_item):
        kv_piece, offset_now = scan_item
        allowed, touched = piece_mask(offset_now)

        def stats_accumulate(state_in):
            peak_now, sum_exp = state_in
            scores = jnp.where(allowed[None], score_block(query_rot, kv_piece[:, 0]), NEGATIVE)
            newest = jnp.maximum(peak_now, jnp.max(scores, axis=-1))
            sum_exp = sum_exp * jnp.exp(peak_now - newest) + jnp.sum(
                jnp.exp(scores - newest[..., None]), axis=-1
            )
            return (newest, sum_exp)

        return (lax.cond(touched, stats_accumulate, keep_state, running), None)

    start_stats = (
        jnp.full((head_count, row_count), NEGATIVE, jnp.float32),
        jnp.zeros((head_count, row_count), jnp.float32),
    )
    (peak_now, sum_exp), unused = lax.scan(stats_step, start_stats, (stacked, shift_table))
    log_total = peak_now + jnp.log(sum_exp)

    def output_step(running, scan_item):
        kv_piece, offset_now = scan_item
        allowed, touched = piece_mask(offset_now)

        def output_accumulate(state_in):
            rounded_sum, remainder = state_in
            attend_prob = jnp.where(
                allowed[None],
                jnp.exp(score_block(query_rot, kv_piece[:, 0]) - log_total[..., None]),
                0.0,
            )
            prob_low = attend_prob.astype(jnp.bfloat16)
            rest_low = (attend_prob - prob_low.astype(jnp.float32)).astype(jnp.bfloat16)
            rounded_sum = rounded_sum + jnp.einsum(
                "hqk,khd->qhd", prob_low, kv_piece[:, 1], preferred_element_type=jnp.float32
            )
            remainder = remainder + jnp.einsum(
                "hqk,khd->qhd", rest_low, kv_piece[:, 1], preferred_element_type=jnp.float32
            )
            return (rounded_sum, remainder)

        return (lax.cond(touched, output_accumulate, keep_state, running), None)

    zero_heads = jnp.zeros((row_count, head_count, HEAD_DIM), jnp.float32)
    (rounded_sum, remainder), unused = lax.scan(
        output_step, (zero_heads, zero_heads), (stacked, shift_table)
    )
    attended_low = rounded_sum.reshape(row_count, model_width).astype(jnp.bfloat16)
    attended_full = rounded_sum + remainder
    projected = (
        jnp.dot(attended_low, output_weight, preferred_element_type=jnp.float32) + output_bias
    )
    hidden = inputs + projected
    normed_two = layer_norm(hidden, second_gain, second_offset)
    normed_two_low = normed_two.astype(jnp.bfloat16)
    expanded = (
        jnp.dot(normed_two_low, expand_weight, preferred_element_type=jnp.float32) + expand_bias
    )
    activated_low = gelu_exact(expanded).astype(jnp.bfloat16)
    reduced = (
        jnp.dot(activated_low, reduce_weight, preferred_element_type=jnp.float32) + reduce_bias
    )
    result = (hidden + reduced).astype(jnp.bfloat16)
    out_grad = cotangent[0]
    out_grad_wide = out_grad.astype(jnp.float32)
    grad_reduce_weight = contract_rows(activated_low, out_grad)
    grad_reduce_bias = jnp.sum(out_grad_wide, axis=0)
    grad_activated = contract_cols(out_grad, reduce_weight)
    grad_expanded = jax.vjp(gelu_exact, expanded)[1](grad_activated)[0]
    grad_expanded_low = grad_expanded.astype(jnp.bfloat16)
    grad_expand_weight = contract_rows(normed_two_low, grad_expanded_low)
    grad_expand_bias = jnp.sum(grad_expanded_low.astype(jnp.float32), axis=0)
    grad_normed_two = contract_cols(grad_expanded_low, expand_weight)
    hidden_part, grad_second_gain, grad_second_offset = jax.vjp(
        layer_norm, hidden, second_gain, second_offset
    )[1](grad_normed_two)
    grad_hidden = out_grad_wide + hidden_part
    grad_hidden_low = grad_hidden.astype(jnp.bfloat16)
    grad_output_weight = contract_rows(attended_low, grad_hidden_low)
    grad_output_bias = jnp.sum(grad_hidden_low.astype(jnp.float32), axis=0)
    grad_attended = (
        contract_cols(grad_hidden_low, output_weight)
        .astype(jnp.bfloat16)
        .reshape(row_count, head_count, HEAD_DIM)
    )
    row_delta = jnp.sum(grad_attended.astype(jnp.float32) * attended_full, axis=-1).T

    def grad_parts(kv_piece, allowed):
        attend_prob = jnp.where(
            allowed[None],
            jnp.exp(score_block(query_rot, kv_piece[:, 0]) - log_total[..., None]),
            0.0,
        )
        grad_prob = jnp.einsum(
            "qhd,khd->hqk", grad_attended, kv_piece[:, 1], preferred_element_type=jnp.float32
        )
        grad_scores = (attend_prob * (grad_prob - row_delta[..., None])).astype(jnp.bfloat16)
        return (attend_prob.astype(jnp.bfloat16), grad_scores)

    def back_step(running, scan_item):
        kv_piece, offset_now = scan_item
        allowed, touched = piece_mask(offset_now)

        def back_accumulate(grad_in):
            prob_low, grad_scores = grad_parts(kv_piece, allowed)
            grad_in = (
                grad_in
                + jnp.einsum(
                    "hqk,khd->qhd", grad_scores, kv_piece[:, 0], preferred_element_type=jnp.float32
                )
                * 0.125
            )
            key_part = (
                jnp.einsum(
                    "hqk,qhd->khd", grad_scores, query_rot, preferred_element_type=jnp.float32
                )
                * 0.125
            )
            value_part = jnp.einsum(
                "hqk,qhd->khd", prob_low, grad_attended, preferred_element_type=jnp.float32
            )
            return (
                grad_in,
                jnp.concatenate(
                    [
                        key_part.reshape(row_count, model_width),
                        value_part.reshape(row_count, model_width),
                    ],
                    axis=1,
                ),
            )

        def skip_piece(grad_in):
            return (grad_in, jnp.zeros((row_count, 2 * model_width), jnp.float32))

        return lax.cond(touched, back_accumulate, skip_piece, running)

    grad_query, partials = lax.scan(back_step, zero_heads, (stacked, shift_table))
    grad_kv = partials[0]
    for index_now in range(1, len(offsets)):
        grad_kv = grad_kv + shifted(
            partials[index_now].astype(jnp.bfloat16), "seq", -offsets[index_now]
        ).astype(jnp.float32)
    grad_kv = grad_kv.reshape(row_count, 2, head_count, HEAD_DIM)

    def unrotate(grad_rotated):

        def turned(inputs_now):
            return rotate(inputs_now, cos_table, sin_table)

        return jax.vjp(turned, query_raw)[1](grad_rotated)[0]

    grad_triple = jnp.stack(
        [unrotate(grad_query), unrotate(grad_kv[:, 0]), grad_kv[:, 1]], axis=1
    ).reshape(row_count, 3 * model_width)
    grad_triple_low = grad_triple.astype(jnp.bfloat16)
    grad_triple_weight = contract_rows(normed_low, grad_triple_low)
    grad_triple_bias = jnp.sum(grad_triple_low.astype(jnp.float32), axis=0)
    grad_query_key_bias = grad_triple_bias[: 2 * model_width]
    grad_value_bias = grad_triple_bias[2 * model_width :]
    grad_normed = contract_cols(grad_triple_low, triple_weight)
    input_part, grad_first_gain, grad_first_offset = jax.vjp(
        layer_norm, inputs, first_gain, first_offset
    )[1](grad_normed)
    input_grad = grad_hidden + input_part
    summed = (
        lax.psum_scatter(grad_first_gain, ("seq", "dp"), scatter_dimension=0, tiled=True),
        lax.psum_scatter(grad_first_offset, ("seq", "dp"), scatter_dimension=0, tiled=True),
        lax.psum_scatter(grad_triple_weight, ("seq", "dp"), scatter_dimension=0, tiled=True),
        lax.psum_scatter(grad_query_key_bias, ("seq", "dp"), scatter_dimension=0, tiled=True),
        lax.psum_scatter(grad_value_bias, ("seq", "dp"), scatter_dimension=0, tiled=True),
        lax.psum_scatter(grad_output_weight, ("seq", "dp"), scatter_dimension=0, tiled=True),
        lax.psum_scatter(grad_output_bias, ("seq", "dp"), scatter_dimension=0, tiled=True),
        lax.psum_scatter(grad_second_gain, ("seq", "dp"), scatter_dimension=0, tiled=True),
        lax.psum_scatter(grad_second_offset, ("seq", "dp"), scatter_dimension=0, tiled=True),
        lax.psum_scatter(grad_expand_weight, ("seq", "dp"), scatter_dimension=0, tiled=True),
        lax.psum_scatter(grad_expand_bias, ("seq", "dp"), scatter_dimension=0, tiled=True),
        lax.psum_scatter(grad_reduce_weight, ("seq", "dp"), scatter_dimension=0, tiled=True),
        lax.psum_scatter(grad_reduce_bias, ("seq", "dp"), scatter_dimension=0, tiled=True),
    )
    return (
        result[None],
        input_grad[None],
        summed[0],
        summed[1],
        summed[2],
        summed[3],
        summed[4],
        summed[5],
        summed[6],
        summed[7],
        summed[8],
        summed[9],
        summed[10],
        summed[11],
        summed[12],
    )


def solution(mesh):
    placed = (
        P("dp", "seq", None),
        P("dp", "seq"),
        P("dp", "seq"),
        P("dp", None, "seq"),
        P(),
        P(),
        P(),
        P(),
        P(),
        P(),
        P(),
        P(),
        P(),
        P(),
        P(),
        P(),
        P("dp", "seq", None),
    )
    return jax.shard_map(
        per_device,
        mesh=mesh,
        in_specs=placed,
        out_specs=(
            P("dp", "seq", None),
            P("dp", "seq", None),
            P(("seq", "dp")),
            P(("seq", "dp")),
            P(("seq", "dp"), None),
            P(("seq", "dp")),
            P(("seq", "dp")),
            P(("seq", "dp"), None),
            P(("seq", "dp")),
            P(("seq", "dp")),
            P(("seq", "dp")),
            P(("seq", "dp"), None),
            P(("seq", "dp")),
            P(("seq", "dp"), None),
            P(("seq", "dp")),
        ),
        check_vma=False,
    )
```

profile of v0, /device:TPU:0, one launch (start us, length us, event | category | flops | bytes accessed | tf_op | source)
XLA Modules:
  0.0 2608.7 jit_solution(17724758041204464958)
XLA Ops:
  13.9 8.0 convolution_add_fusion
  35.6 20.9 concatenate.20
  70.9 6.6 collective-permute-start.10
  85.2 21.9 collective-permute-done.12
  110.7 17.3 collective-permute-start.6
  128.0 47.4 %collective-permute-done.10 = bf16[392,2048]{1,0:T(8,128)(2,1)} collective-permute-done((bf16[392,2048]{1,0:T(8,128)(2,1)}, bf16[392,2048]{1,0:T(8,128)(2,1)}, u32[]{:S(2)}, u32[]{:S(2)}) %collective-permute-start.10) | collective-permute-done | bytes 1605664 | tf_op jit(solution)/shard_map/ppermute | solution.py:20
  176.7 24.5 collective-permute-start.4
  201.3 8.6 collective-permute-done.8
  213.6 30.7 %collective-permute-done.6 = bf16[392,2048]{1,0:T(8,128)(2,1)} collective-permute-done((bf16[392,2048]{1,0:T(8,128)(2,1)}, bf16[392,2048]{1,0:T(8,128)(2,1)}, u32[]{:S(2)}, u32[]{:S(2)}) %collective-permute-start.6) | collective-permute-done | bytes 1605664 | tf_op jit(solution)/shard_map/ppermute | solution.py:20
  252.1 15.7 concatenate.22
  348.9 32.2 %collective-permute-done.13 = bf16[392,2048]{1,0:T(8,128)(2,1)} collective-permute-done((bf16[392,2048]{1,0:T(8,128)(2,1)}, bf16[392,2048]{1,0:T(8,128)(2,1)}, u32[]{:S(2)}, u32[]{:S(2)}) %collective-permute-start.13) | collective-permute-done | bytes 1605664 | tf_op jit(solution)/shard_map/ppermute | solution.py:20
  388.7 68.8 %while.45 = (s32[]{:T(128)}, f32[16,392]{1,0:T(8,128)S(1)}, f32[16,392]{1,0:T(8,128)}, bf16[15,392,2,16,64]{1,4,3,2,0:T(8,128)(2,1)}, bf16[392,16,64]{0,2,1:T(8,...) while((s32[]{:T(128)}, f32[16,392]{1,0:T(8,128)S(1)}, ...), condition=%wide.region_8.9_spmd.clone.clone, body=%wide.region_2.8_spmd.sunk.clone.clone.sunk | while | flops 332541824 | bytes 26034564 | solution.py:166
  392.0 9.6 conditional.15
  408.1 9.6 conditional.15
  461.4 96.1 %while.46 = (s32[]{:T(128)}, f32[392,16,64]{0,2,1:T(8,128)}, f32[392,16,64]{0,2,1:T(8,128)}, bf16[15,392,2,16,64]{1,4,3,2,0:T(8,128)(2,1)}, bf16[392,16,64]{0,2,...) while((s32[]{:T(128)}, f32[392,16,64]{0,2,1:T(8,128)}, ...), condition=%wide.region_13.14_spmd.clone.clone, body=%wide.region_9.13_spmd.sunk.clone.clone.sunk | while | flops 972574336 | bytes 70647696 | solution.py:193
  464.9 23.1 conditional.16
  473.2 6.6 bitcast_add_fusion
  479.9 6.8 bitcast_add_fusion.1
  494.6 23.1 conditional.16
  502.9 6.6 bitcast_add_fusion
  509.6 6.8 bitcast_add_fusion.1
  561.0 21.6 multiply_convert_fusion
  582.6 15.0 convert_reduce_fusion
  617.7 280.7 %while.47 = (s32[]{:T(128)}, f32[392,16,64]{0,2,1:T(8,128)}, f32[15,392,2048]{2,1,0:T(8,128)}, bf16[15,392,2,16,64]{1,4,3,2,0:T(8,128)(2,1)}, bf16[392,16,64]{0,...) while((s32[]{:T(128)}, f32[392,16,64]{0,2,1:T(8,128)}, ...), condition=%wide.region_23.24_spmd.clone.clone, body=%wide.region_19.23_spmd.sunk.clone.clone.sunk | while | flops 1600727680 | bytes 85343096 | solution.py:286
  621.1 30.6 %conditional.17 = (f32[392,16,64]{0,2,1:T(8,128)}, f32[1,392,2048]{1,2,0:T(8,128)}) conditional(s32[]{:T(128)} %convert_element_type.422, f32[392,16,64]{0,2,1:T(8,128)} %get-tuple-element.969, (pred[392,392]{0,1:T(8,128)(4,1)S(1)}, bf16[15,392,2,16,64]{1,4,3,2,0:T(8,128)(2,1)}, s32[]{:T(128)}, bf16[392,16,64]{0,2,1:T(8,128)(2,1)S(1)}, ...), branch_computations={%region_21.21_spmd, %region_22.22_spmd} | conditional | flops 1600112640 | bytes 72321648 | solution.py:284
  623.0 6.6 fusion.41
  635.7 7.2 fusion.36
  679.1 30.6 %conditional.17 = (f32[392,16,64]{0,2,1:T(8,128)}, f32[1,392,2048]{1,2,0:T(8,128)}) conditional(s32[]{:T(128)} %convert_element_type.422, f32[392,16,64]{0,2,1:T(8,128)} %get-tuple-element.969, (pred[392,392]{0,1:T(8,128)(4,1)S(1)}, bf16[15,392,2,16,64]{1,4,3,2,0:T(8,128)(2,1)}, s32[]{:T(128)}, bf16[392,16,64]{0,2,1:T(8,128)(2,1)S(1)}, ...), branch_computations={%region_21.21_spmd, %region_22.22_spmd} | conditional | flops 1600112640 | bytes 72321648 | solution.py:284
  693.7 7.2 fusion.36
  898.4 25.1 convert.68
  923.5 13.9 slice_bitcast_fusion.28
  938.7 420.1 %collective-permute-start.27 = (bf16[392,2048]{1,0:T(8,128)(2,1)}, bf16[392,2048]{1,0:T(8,128)(2,1)S(1)}, u32[]{:S(2)}, u32[]{:S(2)}) collective-permute-start(bf16[392,2048]{1,0:T(8,128)(2,1)} %get-tuple-element.603), channel_id=1, source_target_pairs={{0,14},{2,16},{4,18},{6,20},{8,22},{10,24},{12,26},{14,28},{16,30}... | collective-permute-start | bytes 4816904 | tf_op jit(solution)/shard_map/ppermute | solution.py:20
  1362.9 16.6 collective-permute-start.23
  1379.5 14.8 collective-permute-done.27
  1395.6 102.2 %collective-permute-start.21 = (bf16[392,2048]{1,0:T(8,128)(2,1)S(1)}, bf16[392,2048]{1,0:T(8,128)(2,1)S(1)}, u32[]{:S(2)}, u32[]{:S(2)}) collective-permute-start(bf16[392,2048]{1,0:T(8,128)(2,1)S(1)} %get-tuple-element.609), channel_id=1, source_target_pairs={{0,8},{2,10},{4,12},{6,14},{8,16},{10,18},{12,20},{14,22},{16,24},... | collective-permute-start | bytes 4816904 | tf_op jit(solution)/shard_map/ppermute | solution.py:20
  1499.2 42.5 %collective-permute-start.19 = (bf16[392,2048]{1,0:T(8,128)(2,1)}, bf16[392,2048]{1,0:T(8,128)(2,1)S(1)}, u32[]{:S(2)}, u32[]{:S(2)}) collective-permute-start(bf16[392,2048]{1,0:T(8,128)(2,1)} %get-tuple-element.611), channel_id=1, source_target_pairs={{0,6},{2,8},{4,10},{6,12},{8,14},{10,16},{12,18},{14,20},{16,22},{... | collective-permute-start | bytes 4816904 | tf_op jit(solution)/shard_map/ppermute | solution.py:20
  1542.9 35.7 %collective-permute-start.17 = (bf16[392,2048]{1,0:T(8,128)(2,1)}, bf16[392,2048]{1,0:T(8,128)(2,1)S(1)}, u32[]{:S(2)}, u32[]{:S(2)}) collective-permute-start(bf16[392,2048]{1,0:T(8,128)(2,1)} %get-tuple-element.613), channel_id=1, source_target_pairs={{0,4},{2,6},{4,8},{6,10},{8,12},{10,14},{12,16},{14,18},{16,20},{1... | collective-permute-start | bytes 4816904 | tf_op jit(solution)/shard_map/ppermute | solution.py:20
  1580.0 29.8 %collective-permute-done.20 = bf16[392,2048]{1,0:T(8,128)(2,1)S(1)} collective-permute-done((bf16[392,2048]{1,0:T(8,128)(2,1)S(1)}, bf16[392,2048]{1,0:T(8,128)(2,1)S(1)}, u32[]{:S(2)}, u32[]{:S(2)}) %collective-permute-start.20) | collective-permute-done | bytes 1605664 | tf_op jit(solution)/shard_map/ppermute | solution.py:20
  1616.6 8.1 fusion.65
  1639.8 7.1 fusion.86
  1648.3 10.3 fusion.114
  1658.8 12.5 fusion.89
  1672.0 8.7 fusion.83
  1680.9 6.9 fusion.116
  1691.2 124.4 %all-reduce.21 = (f32[1024]{0:T(1024)S(1)}, f32[1024]{0:T(1024)S(1)}, f32[2048]{0:T(1024)S(1)}, f32[1024]{0:T(1024)S(1)}, f32[1024]{0:T(1024)S(1)}, /*index=5*/f...) all-reduce(f32[1024]{0:T(1024)S(1)} %get-tuple-element.516, ...), channel_id=2, replica_groups=mesh['seq'=16,'dp'=2] {'seq','dp'}, use_global_device_ids=true, to_apply=%region_27.28.clone | all-reduce | flops 13312 | bytes 106496
  1820.8 60.4 %reduce-scatter.5.cloned.1.call-done = f32[32,3072]{1,0:T(8,128)} async-done(((f32[1024,3072]{1,0:T(8,128)}), f32[32,3072]{1,0:T(8,128)}) %reduce-scatter.5.cloned.1.call-update) | async-done | bytes 393232 | tf_op jit(solution)/shard_map/reduce_scatter | solution.py:317
  1881.2 359.4 %reduce-scatter.9.cloned.1.call-done = f32[32,4096]{1,0:T(8,128)} async-done(((f32[1024,4096]{1,0:T(8,128)}), f32[32,4096]{1,0:T(8,128)}) %reduce-scatter.9.cloned.1.call-update) | async-done | bytes 524304 | tf_op jit(solution)/shard_map/reduce_scatter | solution.py:324
  2240.7 361.3 %reduce-scatter.11.cloned.1.call-done = f32[128,1024]{1,0:T(8,128)} async-done(((f32[4096,1024]{1,0:T(8,128)}), f32[128,1024]{1,0:T(8,128)}) %reduce-scatter.11.cloned.1.call-update) | async-done | bytes 524304 | tf_op jit(solution)/shard_map/reduce_scatter | solution.py:326
  (828 shorter events, 587.6 us)
Async XLA Ops:
  7.2 552.2 %copy-start = (bf16[1024,1024]{1,0:T(8,128)(2,1)S(1)}, bf16[1024,1024]{1,0:T(8,128)(2,1)}, u32[]{:S(2)}) copy-start(bf16[1024,1024]{1,0:T(8,128)(2,1)} %param.38) | copy-start | bytes 6291460
  7.2 1813.6 %reduce-scatter.7.cloned.1.call-start = ((), (), s32[]{:S(2)}) async-start(), calls=%async_computation.5 | async-start | bytes 4325376 | tf_op jit(solution)/shard_map/reduce_scatter | solution.py:320
  9.8 239.1 %copy-start.33 = (f32[392,11]{0,1:T(8,128)}, f32[392,11]{0,1:T(8,128)S(1)}, u32[]{:S(2)}) copy-start(f32[392,11]{0,1:T(8,128)S(1)} %get-tuple-element.658) | copy-start | bytes 51748
  9.8 239.1 %copy-start.35 = (f32[392,11]{0,1:T(8,128)}, f32[392,11]{0,1:T(8,128)S(1)}, u32[]{:S(2)}) copy-start(f32[392,11]{0,1:T(8,128)S(1)} %get-tuple-element.659) | copy-start | bytes 51748
  9.8 239.1 %copy-start.37 = (f32[392,11]{0,1:T(8,128)}, f32[392,11]{0,1:T(8,128)S(1)}, u32[]{:S(2)}) copy-start(f32[392,11]{0,1:T(8,128)S(1)} %get-tuple-element.676) | copy-start | bytes 51748
  9.8 239.1 %copy-start.39 = (f32[392,11]{0,1:T(8,128)}, f32[392,11]{0,1:T(8,128)S(1)}, u32[]{:S(2)}) copy-start(f32[392,11]{0,1:T(8,128)S(1)} %get-tuple-element.677) | copy-start | bytes 51748
  63.1 43.9 %collective-permute-start.12 = (bf16[392,2048]{1,0:T(8,128)(2,1)}, bf16[392,2048]{1,0:T(8,128)(2,1)}, u32[]{:S(2)}, u32[]{:S(2)}) collective-permute-start(bf16[392,2048]{1,0:T(8,128)(2,1)} %copy.94), channel_id=1, source_target_pairs={{0,14},{2,16},{4,18},{6,20},{8,22},{10,24},{12,26},{14,28},{16,30}... | collective-permute-start | bytes 4816904 | tf_op jit(solution)/shard_map/ppermute | solution.py:20
  69.6 41.1 %collective-permute-start.11 = (bf16[392,2048]{1,0:T(8,128)(2,1)}, bf16[392,2048]{1,0:T(8,128)(2,1)}, u32[]{:S(2)}, u32[]{:S(2)}) collective-permute-start(bf16[392,2048]{1,0:T(8,128)(2,1)} %copy.94), channel_id=1, source_target_pairs={{12,0},{14,2},{16,4},{18,6},{20,8},{22,10},{24,12},{26,14},{28,16}... | collective-permute-start | bytes 4816904 | tf_op jit(solution)/shard_map/ppermute | solution.py:20
  70.9 104.5 %collective-permute-start.10 = (bf16[392,2048]{1,0:T(8,128)(2,1)}, bf16[392,2048]{1,0:T(8,128)(2,1)}, u32[]{:S(2)}, u32[]{:S(2)}) collective-permute-start(bf16[392,2048]{1,0:T(8,128)(2,1)} %copy.94), channel_id=1, source_target_pairs={{0,12},{2,14},{4,16},{6,18},{8,20},{10,22},{12,24},{14,26},{16,28}... | collective-permute-start | bytes 4816904 | tf_op jit(solution)/shard_map/ppermute | solution.py:20
  77.5 99.2 %collective-permute-start.9 = (bf16[392,2048]{1,0:T(8,128)(2,1)}, bf16[392,2048]{1,0:T(8,128)(2,1)}, u32[]{:S(2)}, u32[]{:S(2)}) collective-permute-start(bf16[392,2048]{1,0:T(8,128)(2,1)} %copy.94), channel_id=1, source_target_pairs={{10,0},{12,2},{14,4},{16,6},{18,8},{20,10},{22,12},{24,14},{26,16}... | collective-permute-start | bytes 4816904 | tf_op jit(solution)/shard_map/ppermute | solution.py:20
  78.8 131.0 %collective-permute-start.8 = (bf16[392,2048]{1,0:T(8,128)(2,1)}, bf16[392,2048]{1,0:T(8,128)(2,1)}, u32[]{:S(2)}, u32[]{:S(2)}) collective-permute-start(bf16[392,2048]{1,0:T(8,128)(2,1)} %copy.94), channel_id=1, source_target_pairs={{0,10},{2,12},{4,14},{6,16},{8,18},{10,20},{12,22},{14,24},{16,26}... | collective-permute-start | bytes 4816904 | tf_op jit(solution)/shard_map/ppermute | solution.py:20
  107.0 105.2 %collective-permute-start.7 = (bf16[392,2048]{1,0:T(8,128)(2,1)}, bf16[392,2048]{1,0:T(8,128)(2,1)}, u32[]{:S(2)}, u32[]{:S(2)}) collective-permute-start(bf16[392,2048]{1,0:T(8,128)(2,1)} %copy.94), channel_id=1, source_target_pairs={{8,0},{10,2},{12,4},{14,6},{16,8},{18,10},{20,12},{22,14},{24,16},... | collective-permute-start | bytes 4816904 | tf_op jit(solution)/shard_map/ppermute | solution.py:20
  110.7 133.5 %collective-permute-start.6 = (bf16[392,2048]{1,0:T(8,128)(2,1)}, bf16[392,2048]{1,0:T(8,128)(2,1)}, u32[]{:S(2)}, u32[]{:S(2)}) collective-permute-start(bf16[392,2048]{1,0:T(8,128)(2,1)} %copy.94), channel_id=1, source_target_pairs={{0,8},{2,10},{4,12},{6,14},{8,16},{10,18},{12,20},{14,22},{16,24},... | collective-permute-start | bytes 4816904 | tf_op jit(solution)/shard_map/ppermute | solution.py:20
  175.4 72.1 %collective-permute-start.5 = (bf16[392,2048]{1,0:T(8,128)(2,1)}, bf16[392,2048]{1,0:T(8,128)(2,1)}, u32[]{:S(2)}, u32[]{:S(2)}) collective-permute-start(bf16[392,2048]{1,0:T(8,128)(2,1)} %copy.94), channel_id=1, source_target_pairs={{6,0},{8,2},{10,4},{12,6},{14,8},{16,10},{18,12},{20,14},{22,16},{... | collective-permute-start | bytes 4816904 | tf_op jit(solution)/shard_map/ppermute | solution.py:20
  176.7 124.2 %collective-permute-start.4 = (bf16[392,2048]{1,0:T(8,128)(2,1)}, bf16[392,2048]{1,0:T(8,128)(2,1)}, u32[]{:S(2)}, u32[]{:S(2)}) collective-permute-start(bf16[392,2048]{1,0:T(8,128)(2,1)} %copy.94), channel_id=1, source_target_pairs={{0,6},{2,8},{4,10},{6,12},{8,14},{10,16},{12,18},{14,20},{16,22},{... | collective-permute-start | bytes 4816904 | tf_op jit(solution)/shard_map/ppermute | solution.py:20
  209.8 96.3 %collective-permute-start.2 = (bf16[392,2048]{1,0:T(8,128)(2,1)}, bf16[392,2048]{1,0:T(8,128)(2,1)}, u32[]{:S(2)}, u32[]{:S(2)}) collective-permute-start(bf16[392,2048]{1,0:T(8,128)(2,1)} %copy.94), channel_id=1, source_target_pairs={{0,4},{2,6},{4,8},{6,10},{8,12},{10,14},{12,16},{14,18},{16,20},{1... | collective-permute-start | bytes 4816904 | tf_op jit(solution)/shard_map/ppermute | solution.py:20
  212.3 97.6 %collective-permute-start.1 = (bf16[392,2048]{1,0:T(8,128)(2,1)}, bf16[392,2048]{1,0:T(8,128)(2,1)}, u32[]{:S(2)}, u32[]{:S(2)}) collective-permute-start(bf16[392,2048]{1,0:T(8,128)(2,1)} %copy.94), channel_id=1, source_target_pairs={{2,0},{4,2},{6,4},{8,6},{10,8},{12,10},{14,12},{16,14},{18,16},{20... | collective-permute-start | bytes 4816904 | tf_op jit(solution)/shard_map/ppermute | solution.py:20
  244.2 69.4 %collective-permute-start = (bf16[392,2048]{1,0:T(8,128)(2,1)}, bf16[392,2048]{1,0:T(8,128)(2,1)}, u32[]{:S(2)}, u32[]{:S(2)}) collective-permute-start(bf16[392,2048]{1,0:T(8,128)(2,1)} %copy.94), channel_id=1, source_target_pairs={{0,2},{2,4},{4,6},{6,8},{8,10},{10,12},{12,14},{14,16},{16,18},{18... | collective-permute-start | bytes 4816904 | tf_op jit(solution)/shard_map/ppermute | solution.py:20
  247.5 77.0 %collective-permute-start.3 = (bf16[392,2048]{1,0:T(8,128)(2,1)}, bf16[392,2048]{1,0:T(8,128)(2,1)}, u32[]{:S(2)}, u32[]{:S(2)}) collective-permute-start(bf16[392,2048]{1,0:T(8,128)(2,1)} %copy.94), channel_id=1, source_target_pairs={{4,0},{6,2},{8,4},{10,6},{12,8},{14,10},{16,12},{18,14},{20,16},{2... | collective-permute-start | bytes 4816904 | tf_op jit(solution)/shard_map/ppermute | solution.py:20
  300.9 80.1 %collective-permute-start.13 = (bf16[392,2048]{1,0:T(8,128)(2,1)}, bf16[392,2048]{1,0:T(8,128)(2,1)}, u32[]{:S(2)}, u32[]{:S(2)}) collective-permute-start(bf16[392,2048]{1,0:T(8,128)(2,1)} %copy.94), channel_id=1, source_target_pairs={{14,0},{16,2},{18,4},{20,6},{22,8},{24,10},{26,12},{28,14},{30,16}... | collective-permute-start | bytes 4816904 | tf_op jit(solution)/shard_map/ppermute | solution.py:20
  348.9 39.8 %copy-start.72 = (s32[15]{0:T(128)S(1)}, s32[15]{0:T(128)}, u32[]{:S(2)}) copy-start(s32[15]{0:T(128)} %constant.206.clone..sunk.9) | copy-start | bytes 184
  559.4 38.1 %slice-start = ((s8[8388608]{0:T(1024)(128)(4,1)}), s8[4194304]{0:T(1024)(128)(4,1)S(1)}, s32[]{:S(2)}) async-start(s8[8388608]{0:T(1024)(128)(4,1)} %bitcast.310), calls=%async_computation.8 | async-start | bytes 8388608
  560.6 43.5 %copy-start.7 = (f32[392,1024]{1,0:T(8,128)}, f32[392,1024]{1,0:T(8,128)S(1)}, u32[]{:S(2)}) copy-start(f32[392,1024]{1,0:T(8,128)S(1)} %get-tuple-element.670) | copy-start | bytes 4816900
  560.6 43.5 %copy-start.50 = (f32[392]{0:T(512)}, f32[392]{0:T(512)S(1)}, u32[]{:S(2)}) copy-start(f32[392]{0:T(512)S(1)} %broadcast_multiply_fusion.3) | copy-start | bytes 4708
  561.0 43.1 %copy-start.59 = (f32[392]{0:T(512)}, f32[392]{0:T(512)S(1)}, u32[]{:S(2)}) copy-start(f32[392]{0:T(512)S(1)} %fusion.106) | copy-start | bytes 4708
  561.0 36.6 %slice-start.1 = ((s8[8388608]{0:T(1024)(128)(4,1)}), s8[4194304]{0:T(1024)(128)(4,1)S(1)}, s32[]{:S(2)}) async-start(s8[8388608]{0:T(1024)(128)(4,1)} %bitcast.310), calls=%async_computation.9 | async-start | bytes 8388608
  613.6 1267.7 %reduce-scatter.5.cloned.1.call-start = ((), (), s32[]{:S(2)}) async-start(), calls=%async_computation.4 | async-start | bytes 12976128 | tf_op jit(solution)/shard_map/reduce_scatter | solution.py:317
  923.5 689.8 %copy-start.34 = (f32[392,11]{0,1:T(8,128)S(1)}, f32[392,11]{0,1:T(8,128)}, u32[]{:S(2)}) copy-start(f32[392,11]{0,1:T(8,128)} %copy-done.33) | copy-start | bytes 51748
  923.5 689.8 %copy-start.36 = (f32[392,11]{0,1:T(8,128)S(1)}, f32[392,11]{0,1:T(8,128)}, u32[]{:S(2)}) copy-start(f32[392,11]{0,1:T(8,128)} %copy-done.35) | copy-start | bytes 51748
  923.5 689.8 %copy-start.38 = (f32[392,11]{0,1:T(8,128)S(1)}, f32[392,11]{0,1:T(8,128)}, u32[]{:S(2)}) copy-start(f32[392,11]{0,1:T(8,128)} %copy-done.37) | copy-start | bytes 51748
  923.5 689.8 %copy-start.40 = (f32[392,11]{0,1:T(8,128)S(1)}, f32[392,11]{0,1:T(8,128)}, u32[]{:S(2)}) copy-start(f32[392,11]{0,1:T(8,128)} %copy-done.39) | copy-start | bytes 51748
  937.4 425.4 %collective-permute-start.14 = (bf16[392,2048]{1,0:T(8,128)(2,1)}, bf16[392,2048]{1,0:T(8,128)(2,1)S(1)}, u32[]{:S(2)}, u32[]{:S(2)}) collective-permute-start(bf16[392,2048]{1,0:T(8,128)(2,1)} %get-tuple-element.602), channel_id=1, source_target_pairs={{2,0},{4,2},{6,4},{8,6},{10,8},{12,10},{14,12},{16,14},{18,16},{20... | collective-permute-start | bytes 4816904 | tf_op jit(solution)/shard_map/ppermute | solution.py:20
  938.7 455.5 %collective-permute-start.27 = (bf16[392,2048]{1,0:T(8,128)(2,1)}, bf16[392,2048]{1,0:T(8,128)(2,1)S(1)}, u32[]{:S(2)}, u32[]{:S(2)}) collective-permute-start(bf16[392,2048]{1,0:T(8,128)(2,1)} %get-tuple-element.603), channel_id=1, source_target_pairs={{0,14},{2,16},{4,18},{6,20},{8,22},{10,24},{12,26},{14,28},{16,30}... | collective-permute-start | bytes 4816904 | tf_op jit(solution)/shard_map/ppermute | solution.py:20
  1358.9 36.7 %collective-permute-start.26 = (bf16[392,2048]{1,0:T(8,128)(2,1)}, bf16[392,2048]{1,0:T(8,128)(2,1)S(1)}, u32[]{:S(2)}, u32[]{:S(2)}) collective-permute-start(bf16[392,2048]{1,0:T(8,128)(2,1)} %get-tuple-element.604), channel_id=1, source_target_pairs={{14,0},{16,2},{18,4},{20,6},{22,8},{24,10},{26,12},{28,14},{30,16}... | collective-permute-start | bytes 4816904 | tf_op jit(solution)/shard_map/ppermute | solution.py:20
  1360.2 137.7 %collective-permute-start.25 = (bf16[392,2048]{1,0:T(8,128)(2,1)}, bf16[392,2048]{1,0:T(8,128)(2,1)S(1)}, u32[]{:S(2)}, u32[]{:S(2)}) collective-permute-start(bf16[392,2048]{1,0:T(8,128)(2,1)} %get-tuple-element.605), channel_id=1, source_target_pairs={{0,12},{2,14},{4,16},{6,18},{8,20},{10,22},{12,24},{14,26},{16,28}... | collective-permute-start | bytes 4816904 | tf_op jit(solution)/shard_map/ppermute | solution.py:20
  1361.6 137.6 %collective-permute-start.24 = (bf16[392,2048]{1,0:T(8,128)(2,1)}, bf16[392,2048]{1,0:T(8,128)(2,1)S(1)}, u32[]{:S(2)}, u32[]{:S(2)}) collective-permute-start(bf16[392,2048]{1,0:T(8,128)(2,1)} %get-tuple-element.606), channel_id=1, source_target_pairs={{12,0},{14,2},{16,4},{18,6},{20,8},{22,10},{24,12},{26,14},{28,16}... | collective-permute-start | bytes 4816904 | tf_op jit(solution)/shard_map/ppermute | solution.py:20
  1362.9 178.8 %collective-permute-start.23 = (bf16[392,2048]{1,0:T(8,128)(2,1)}, bf16[392,2048]{1,0:T(8,128)(2,1)S(1)}, u32[]{:S(2)}, u32[]{:S(2)}) collective-permute-start(bf16[392,2048]{1,0:T(8,128)(2,1)} %get-tuple-element.607), channel_id=1, source_target_pairs={{0,10},{2,12},{4,14},{6,16},{8,18},{10,20},{12,22},{14,24},{16,26}... | collective-permute-start | bytes 4816904 | tf_op jit(solution)/shard_map/ppermute | solution.py:20
  1394.3 148.7 %collective-permute-start.22 = (bf16[392,2048]{1,0:T(8,128)(2,1)S(1)}, bf16[392,2048]{1,0:T(8,128)(2,1)S(1)}, u32[]{:S(2)}, u32[]{:S(2)}) collective-permute-start(bf16[392,2048]{1,0:T(8,128)(2,1)S(1)} %get-tuple-element.608), channel_id=1, source_target_pairs={{10,0},{12,2},{14,4},{16,6},{18,8},{20,10},{22,12},{24,14},{26,16}... | collective-permute-start | bytes 4816904 | tf_op jit(solution)/shard_map/ppermute | solution.py:20
  1395.6 183.1 %collective-permute-start.21 = (bf16[392,2048]{1,0:T(8,128)(2,1)S(1)}, bf16[392,2048]{1,0:T(8,128)(2,1)S(1)}, u32[]{:S(2)}, u32[]{:S(2)}) collective-permute-start(bf16[392,2048]{1,0:T(8,128)(2,1)S(1)} %get-tuple-element.609), channel_id=1, source_target_pairs={{0,8},{2,10},{4,12},{6,14},{8,16},{10,18},{12,20},{14,22},{16,24},... | collective-permute-start | bytes 4816904 | tf_op jit(solution)/shard_map/ppermute | solution.py:20
  1497.8 111.9 %collective-permute-start.20 = (bf16[392,2048]{1,0:T(8,128)(2,1)S(1)}, bf16[392,2048]{1,0:T(8,128)(2,1)S(1)}, u32[]{:S(2)}, u32[]{:S(2)}) collective-permute-start(bf16[392,2048]{1,0:T(8,128)(2,1)S(1)} %get-tuple-element.610), channel_id=1, source_target_pairs={{8,0},{10,2},{12,4},{14,6},{16,8},{18,10},{20,12},{22,14},{24,16},... | collective-permute-start | bytes 4816904 | tf_op jit(solution)/shard_map/ppermute | solution.py:20
  1499.2 117.4 %collective-permute-start.19 = (bf16[392,2048]{1,0:T(8,128)(2,1)}, bf16[392,2048]{1,0:T(8,128)(2,1)S(1)}, u32[]{:S(2)}, u32[]{:S(2)}) collective-permute-start(bf16[392,2048]{1,0:T(8,128)(2,1)} %get-tuple-element.611), channel_id=1, source_target_pairs={{0,6},{2,8},{4,10},{6,12},{8,14},{10,16},{12,18},{14,20},{16,22},{... | collective-permute-start | bytes 4816904 | tf_op jit(solution)/shard_map/ppermute | solution.py:20
  1541.6 74.9 %collective-permute-start.18 = (bf16[392,2048]{1,0:T(8,128)(2,1)}, bf16[392,2048]{1,0:T(8,128)(2,1)S(1)}, u32[]{:S(2)}, u32[]{:S(2)}) collective-permute-start(bf16[392,2048]{1,0:T(8,128)(2,1)} %get-tuple-element.612), channel_id=1, source_target_pairs={{6,0},{8,2},{10,4},{12,6},{14,8},{16,10},{18,12},{20,14},{22,16},{... | collective-permute-start | bytes 4816904 | tf_op jit(solution)/shard_map/ppermute | solution.py:20
  1542.9 73.6 %collective-permute-start.17 = (bf16[392,2048]{1,0:T(8,128)(2,1)}, bf16[392,2048]{1,0:T(8,128)(2,1)S(1)}, u32[]{:S(2)}, u32[]{:S(2)}) collective-permute-start(bf16[392,2048]{1,0:T(8,128)(2,1)} %get-tuple-element.613), channel_id=1, source_target_pairs={{0,4},{2,6},{4,8},{6,10},{8,12},{10,14},{12,16},{14,18},{16,20},{1... | collective-permute-start | bytes 4816904 | tf_op jit(solution)/shard_map/ppermute | solution.py:20
  1578.7 37.9 %collective-permute-start.16 = (bf16[392,2048]{1,0:T(8,128)(2,1)}, bf16[392,2048]{1,0:T(8,128)(2,1)S(1)}, u32[]{:S(2)}, u32[]{:S(2)}) collective-permute-start(bf16[392,2048]{1,0:T(8,128)(2,1)} %get-tuple-element.614), channel_id=1, source_target_pairs={{4,0},{6,2},{8,4},{10,6},{12,8},{14,10},{16,12},{18,14},{20,16},{2... | collective-permute-start | bytes 4816904 | tf_op jit(solution)/shard_map/ppermute | solution.py:20
  1609.8 6.8 collective-permute-start.15
  1646.9 593.8 %reduce-scatter.9.cloned.1.call-start = ((), (), s32[]{:S(2)}) async-start(), calls=%async_computation.6 | async-start | bytes 17301504 | tf_op jit(solution)/shard_map/reduce_scatter | solution.py:324
  1658.6 943.4 %reduce-scatter.11.cloned.1.call-start = ((), (), s32[]{:S(2)}) async-start(), calls=%async_computation.7 | async-start | bytes 17301504 | tf_op jit(solution)/shard_map/reduce_scatter | solution.py:326
  1688.7 913.4 %copy-start.1 = (bf16[1024,1024]{1,0:T(8,128)(2,1)S(1)}, bf16[1024,1024]{1,0:T(8,128)(2,1)}, u32[]{:S(2)}) copy-start(bf16[1024,1024]{1,0:T(8,128)(2,1)} %param.38) | copy-start | bytes 6291460
  (66 other events, 234.8 us)
Sparse Core Ops, SparseCore 0:
  613.7 397.9 reduce-scatter.6
  1647.0 234.1 reduce-scatter.4
  1884.2 356.4 reduce-scatter.8
  2243.5 358.4 reduce-scatter.10
where the time goes:
time: 2630 us; the launch traced here: 2610 us
  waiting for transfers between devices  969 us (37%)
  starting transfers between devices  708 us (27%)
  local copies, waits for them, and re-layouts  413 us (16%)
  matrix products  200 us (8%)
  blocking collectives  124 us (5%)
  other arithmetic  119 us (5%)
  loops' own time  60.8 us (2%)
    ppermute x28, starting transfers between devices, shifted(): return lax.ppermute(shard, axis, pairs)  707 us
    reduce_scatter x1, waiting for transfers between devices, per_device(): lax.psum_scatter(grad_reduce_weight, ('seq', 'dp'), scatter_dimension=0,...  361 us
    reduce_scatter x1, waiting for transfers between devices, per_device(): lax.psum_scatter(grad_expand_weight, ('seq', 'dp'), scatter_dimension=0,...  359 us
    ppermute x28, waiting for transfers between devices, shifted(): return lax.ppermute(shard, axis, pairs)  188 us
    dynamic_update_slice x30, local copies, waits for them, and re-layouts, per_device(): lax.scan(back_step, zero_heads, (stacked, shift_table))  138 us
    unnamed x1, blocking collectives  124 us
    reduce_scatter x1, waiting for transfers between devices, per_device(): lax.psum_scatter(grad_triple_weight, ('seq', 'dp'), scatter_dimension=0,...  60.4 us
  transfers between devices with their start and end apart: 32, of which 11 were waited for; matrix products, arithmetic and copies ran while one was open for 18% of the time, Pallas kernels for 0%

commit v1 on v0

v1 whole, which is shorter than its diff:
```python
import jax
import jax.numpy as jnp
from jax import lax
from jax.experimental import pallas as pl
from jax.experimental.pallas import tpu as pltpu
from jax.sharding import PartitionSpec as P

HEAD_DIM = 64
CLIP_MIN = 4
CLIP_MAX = 16
EPSILON = 1e-06
MASKED = 1e30
SECTIONS = ((0, 10), (20, 11), (42, 11))
LANES = 128
F32 = jnp.float32
BF16 = jnp.bfloat16
VMEM_LIMIT = 63 * 2**20
Q_TILE = 256
SAFE_ABOVE = 60.0
BACK_SHARE = (3, 4)


def dot(left, right):
    return jnp.dot(left, right, preferred_element_type=F32)


def dot_cols(left, right):
    return lax.dot_general(left, right, (((1,), (1,)), ((), ())), preferred_element_type=F32)


def dot_rows(left, right):
    return lax.dot_general(left, right, (((0,), (0,)), ((), ())), preferred_element_type=F32)


def cost(micros):
    return pl.CostEstimate(flops=int(micros * 1.15e9), bytes_accessed=2**20, transcendentals=0)


def params(**more):
    return pltpu.CompilerParams(vmem_limit_bytes=VMEM_LIMIT, **more)


def lane_index(shape):
    return lax.broadcasted_iota(jnp.int32, shape, len(shape) - 1)


def swap_halves(pair):
    return pltpu.roll(pair, HEAD_DIM, 1)


def rotate_pair(pair, cos_lanes, sin_lanes, inverse):
    lane = lane_index((1, LANES)) % HEAD_DIM
    sign = -1.0 if inverse else 1.0
    total = pair * cos_lanes
    for half in (10, 11):
        first = jnp.zeros(lane.shape, jnp.bool_)
        second = jnp.zeros(lane.shape, jnp.bool_)
        for begin_at, count in SECTIONS:
            if count == half:
                first = first | ((lane >= begin_at) & (lane < begin_at + half))
                second = second | ((lane >= begin_at + half) & (lane < begin_at + 2 * half))
        minus = jnp.where(first, -sign, 0.0)
        plus = jnp.where(second, sign, 0.0)
        total = total + pltpu.roll(pair, LANES - half, 1) * (sin_lanes * minus)
        total = total + pltpu.roll(pair, half, 1) * (sin_lanes * plus)
    return total


def lane_tables(positions):
    angles = jnp.zeros((positions.shape[1], LANES), F32)
    for section, (begin_at, count) in enumerate(SECTIONS):
        frequency = jnp.power(10000.0, -jnp.arange(count, dtype=F32) / count)
        in_head = jnp.zeros((HEAD_DIM,), F32)
        in_head = in_head.at[begin_at : begin_at + count].set(frequency)
        in_head = in_head.at[begin_at + count : begin_at + 2 * count].set(frequency)
        lanes = jnp.tile(in_head, LANES // HEAD_DIM)
        angles = angles + positions[section].astype(F32)[:, None] * lanes[None, :]
    return jnp.cos(angles), jnp.sin(angles)


def all_turns(places):
    spots = jnp.arange(16)
    table = []
    for section in range(len(SECTIONS)):
        only = jnp.where(jnp.arange(len(SECTIONS))[:, None] == section, spots[None, :], 0)
        cos, sin = lane_tables(only)
        lane = jnp.arange(LANES)
        begin_at, count = SECTIONS[section]
        inside = (lane % HEAD_DIM >= begin_at) & (lane % HEAD_DIM < begin_at + 2 * count)
        table.append(jnp.where(inside, jnp.where(lane < HEAD_DIM, cos, sin), 0.0))
    table = jnp.concatenate(table, axis=0)
    hit = places.astype(jnp.int32).transpose(0, 2, 1)[..., None] == spots
    hit = hit.reshape(hit.shape[:2] + table.shape[:1]).astype(F32)
    hit = jnp.pad(hit, ((0, 0), (0, -hit.shape[1] % 16), (0, 0))).reshape(-1, table.shape[0])
    return jnp.dot(hit, table, precision=lax.Precision.HIGHEST)


def slab_bounds(clip_start, frames, first_slab, group_slabs):
    slab_index = first_slab + jnp.arange(clip_start.shape[-1], dtype=jnp.int32)
    unit_base = slab_index // CLIP_MIN * CLIP_MIN
    lower_slab = jnp.maximum(
        jnp.maximum(jnp.minimum(clip_start, slab_index), unit_base - (CLIP_MAX - CLIP_MIN)), 0
    )
    upper_slab = jnp.minimum(
        jnp.minimum(jnp.maximum(clip_start + frames // 2, slab_index + 1), unit_base + CLIP_MAX),
        group_slabs,
    )
    return lower_slab, upper_slab


def norm_parts(rows):
    centred = rows - jnp.mean(rows, axis=-1, keepdims=True)
    spread = jnp.mean(centred * centred, axis=-1, keepdims=True)
    scale = lax.rsqrt(spread + EPSILON)
    return centred * scale, scale


def norm_back(grad, rows, gain):
    unit, scale = norm_parts(rows)
    inner = grad * gain
    part = scale * (
        inner
        - jnp.mean(inner, axis=-1, keepdims=True)
        - unit * jnp.mean(inner * unit, axis=-1, keepdims=True)
    )
    return part, jnp.sum(grad * unit, axis=0, keepdims=True), jnp.sum(grad, axis=0, keepdims=True)


class Sizes:
    def __init__(self, rows, width, ff, n, m, slabs):
        self.rows = rows
        self.width = width
        self.ff = ff
        self.n = n
        self.m = m
        self.heads = width // HEAD_DIM
        self.rep = n // self.heads
        self.shards = n * m
        self.per_unit = CLIP_MIN // slabs
        self.units = n // self.per_unit
        self.slot = (rows + 15) // 16 * 16
        self.unit_rows = self.slot * self.per_unit
        self.tokens = self.slot * n
        self.fold = (rows // 2 + 15) // 16 * 16
        self.rest = rows - self.fold
        self.msg = self.slot + self.fold


def pad_rows(block, count):
    if block.shape[0] == count:
        return block
    return jnp.concatenate([block, jnp.zeros((count - block.shape[0], block.shape[1]), F32)], axis=0)


def fold_head(block, sz, right):
    low = block[: sz.fold]
    high = pad_rows(block[sz.fold :], sz.fold)
    left = lane_index(low.shape) < HEAD_DIM
    if right:
        folded = jnp.where(left, swap_halves(low), high)
    else:
        folded = jnp.where(left, low, swap_halves(high))
    return folded


def project_kernel(sz, tok, gain, offset, wq, wk, wv, bq, bk, bv, cos, sin, meta, msg, normed_out):
    step = pl.program_id(0)

    @pl.when(step == 0)
    def _():
        unit, _ = norm_parts(tok[...].astype(F32))
        normed_out[...] = (unit * gain[...] + offset[...]).astype(BF16)

    normed = normed_out[...]
    query = dot(normed, wq[...]) + bq[...]
    key = dot(normed, wk[...]) + bk[...]
    value = dot(normed, wv[...]) + bv[...]
    left = lane_index((sz.rows, LANES)) < HEAD_DIM
    spare = sz.slot - sz.rows
    facts = jnp.concatenate([jnp.zeros((sz.fold - 8, LANES), F32), meta[...]], axis=0)
    for pair in range(query.shape[1] // LANES):
        cols = slice(pair * LANES, (pair + 1) * LANES)
        q_pair = rotate_pair(query[:, cols], cos[...], sin[...], False) * 0.125
        k_pair = rotate_pair(key[:, cols], cos[...], sin[...], False)
        v_pair = value[:, cols]
        both = (jnp.where(left, k_pair, swap_halves(v_pair)), jnp.where(left, swap_halves(k_pair), v_pair))
        for head in range(2):
            tail = jnp.where(left[:spare], both[head][sz.rows - spare :], 0.0)
            folded = fold_head(q_pair, sz, head == 1) + facts
            rows = jnp.concatenate([both[head], tail, folded], axis=0)
            msg[2 * pair + head] = rows.astype(BF16)


def project(sz, tokens, gain, offset, weight, bias, cos, sin, meta):
    cols = 256
    steps = sz.width // cols
    whole = lambda shape: pl.BlockSpec(shape, lambda j: (0,) * len(shape))
    part = lambda k: pl.BlockSpec((sz.width, cols), lambda j: (0, k * steps + j))
    part_bias = lambda k: pl.BlockSpec((1, cols), lambda j: (0, k * steps + j))
    heads = cols // HEAD_DIM
    return pl.pallas_call(
        lambda *refs: project_kernel(sz, *refs),
        grid=(steps,),
        in_specs=[whole((sz.rows, sz.width)), whole((1, sz.width)), whole((1, sz.width))]
        + [part(0), part(1), part(2), part_bias(0), part_bias(1), part_bias(2)]
        + [whole((sz.rows, LANES)), whole((sz.rows, LANES)), whole((8, LANES))],
        out_specs=[
            pl.BlockSpec((heads, sz.msg, LANES), lambda j: (j, 0, 0)),
            whole((sz.rows, sz.width)),
        ],
        out_shape=[
            jax.ShapeDtypeStruct((sz.heads, sz.msg, LANES), BF16),
            jax.ShapeDtypeStruct((sz.rows, sz.width), BF16),
        ],
        compiler_params=params(),
        cost_estimate=cost(8),
        name="project",
    )(tokens, gain, offset, weight, weight, weight, bias, bias, bias, cos, sin, meta)


def unfold_slot(folded, sz, right):
    wide = folded.astype(F32)
    left = lane_index(wide.shape) < HEAD_DIM
    keep = ~left if right else left
    swapped = swap_halves(wide)
    low, high = (swapped, wide) if right else (wide, swapped)
    return (
        jnp.where(keep, low, 0.0).astype(BF16),
        jnp.where(keep, high, 0.0)[: sz.slot - sz.fold].astype(BF16),
    )


def unfold_into(target, at, folded, sz, right):
    low, high = unfold_slot(folded, sz, right)
    target[pl.ds(at, sz.fold), :] = low
    target[pl.ds(at + sz.fold, sz.slot - sz.fold), :] = high


def loop(count, body):
    def step(index, carry):
        body(index)
        return carry

    lax.fori_loop(0, count, step, 0)


def attend_kernel(sz, first, count, recv, out, kept, qs, kvs, ones_v):
    def unpack(src):
        at = pl.multiple_of(src * sz.slot, 16)
        unfold_into(qs, at, recv[src, sz.slot :, :], sz, False)
        kv = recv[src, 0 : sz.slot, :]
        kvs[pl.ds(at, sz.slot), :] = kv
        left = lane_index((1, LANES)) < HEAD_DIM
        real = lax.broadcasted_iota(jnp.int32, (sz.slot, 1), 0) < sz.rows
        one = jnp.where(real, 1.0, 0.0)
        ones_v[pl.ds(at, sz.slot), :] = jnp.where(left, one, kv.astype(F32)).astype(BF16)

    loop(sz.n, unpack)
    qs[sz.tokens :, :] = jnp.zeros((Q_TILE, LANES), BF16)
    kept[sz.tokens :, :] = jnp.zeros((Q_TILE, LANES), F32)

    def one(unit):
        rows = pl.ds(pl.multiple_of(unit * sz.unit_rows, 16), sz.unit_rows)
        begin = pl.multiple_of(first[unit] * sz.unit_rows, 16)

        def keep(shift, mixed):
            total = mixed[:, 0:1]
            left = lane_index((1, LANES)) < HEAD_DIM
            kept[rows, :] = jnp.where(left, shift + jnp.log(total), mixed * (1.0 / total))

        for span in (1, 2, 4):

            @pl.when(count[unit] == span)
            def _():
                clip = pl.ds(begin, span * sz.unit_rows)
                some = dot_cols(qs[rows, :], kvs[pl.ds(begin, 2 * LANES), :])
                shift = jnp.max(some, axis=1, keepdims=True)
                scores = dot_cols(qs[rows, :], kvs[clip, :])
                prob = jnp.exp(scores - shift).astype(BF16)
                keep(shift, dot(prob, ones_v[clip, :]))
                above = jnp.max(jnp.max(scores, axis=1, keepdims=True) - shift)

                @pl.when(above > SAFE_ABOVE)
                def _():
                    scores = dot_cols(qs[rows, :], kvs[clip, :])
                    peak = jnp.max(scores, axis=1, keepdims=True)
                    prob = jnp.exp(scores - peak).astype(BF16)
                    keep(peak, dot(prob, ones_v[clip, :]))

    loop(sz.units, one)

    def pack(src):
        at = pl.multiple_of(src * sz.slot, 16)
        out[src] = fold_head(kept[pl.ds(at, sz.slot), :][: sz.rows], sz, True).astype(BF16)
        left = lane_index((sz.slot - sz.rows, LANES)) < HEAD_DIM
        kept[pl.ds(at + sz.rows, sz.slot - sz.rows), :] = jnp.where(left, MASKED, 0.0)

    loop(sz.n, pack)


def attend(sz, first, count, recv):
    smem = pl.BlockSpec(memory_space=pltpu.SMEM)
    vmem = pl.BlockSpec(memory_space=pltpu.VMEM)
    shape = jax.ShapeDtypeStruct
    return pl.pallas_call(
        lambda *refs: attend_kernel(sz, *refs),
        in_specs=[smem, smem, vmem],
        out_specs=[vmem] * 4,
        out_shape=[
            shape((sz.n, sz.fold, LANES), BF16),
            shape((sz.tokens + Q_TILE, LANES), F32),
            shape((sz.tokens + Q_TILE, LANES), BF16),
            shape((sz.tokens, LANES), BF16),
        ],
        scratch_shapes=[pltpu.VMEM((sz.tokens, LANES), BF16)],
        compiler_params=params(),
        cost_estimate=cost(32),
        name="attend",
    )(first, count, recv)


def back_tiles(sz, part, first, count, qs, kvs, dos, kept, grad_q, grad_kv, key_t):
    def one(unit):
        begin = pl.multiple_of(unit * sz.unit_rows, 16)
        for span in (1, 2, 4):

            @pl.when((count[unit] == span) & (first[unit] == unit))
            def _():
                length = span * sz.unit_rows
                clip = pl.ds(begin, length)
                turned = kvs[clip, :].astype(F32).T[:HEAD_DIM]
                real = lax.rem(lane_index((1, length)), sz.slot) < sz.rows
                key_t[:, 0:length] = jnp.where(real, turned, 0.0).astype(BF16)

                def q_tile(t, carry):
                    rows = pl.ds(pl.multiple_of(begin + t * Q_TILE, 16), Q_TILE)
                    query = qs[rows, :]
                    grad = dos[rows, :]
                    kept_rows = kept[rows, :]
                    left = lane_index((Q_TILE, LANES)) < HEAD_DIM
                    turned = jnp.where(left, kept_rows, kept_rows * grad.astype(F32)).T
                    inside = lane_index((1, Q_TILE)) < length - t * Q_TILE
                    log_total = jnp.where(inside, turned[0:1, :], MASKED)
                    delta = jnp.sum(turned[HEAD_DIM:, :], axis=0, keepdims=True)
                    keys = kvs[clip, :]
                    prob = jnp.exp(dot_cols(keys, query) - log_total)
                    grad_prob = dot_cols(keys, grad)
                    grad_scores = (prob * (grad_prob - delta)).astype(BF16)
                    grad_kv[clip, :] += dot(grad_scores, query) + dot(prob.astype(BF16), grad)
                    grad_query = dot(key_t[:, 0:length], grad_scores) * 0.125
                    grad_query = jnp.concatenate([grad_query, jnp.zeros_like(grad_query)], axis=0).T
                    if part == 1:
                        own = lax.broadcasted_iota(jnp.int32, (Q_TILE, 1), 0) < length - t * Q_TILE
                        grad_query = jnp.where(own, grad_query, grad_q[rows, :])
                    grad_q[rows, :] = grad_query
                    return carry

                tiles = (length + Q_TILE - 1) // Q_TILE
                middle = (tiles * BACK_SHARE[0] + BACK_SHARE[1] - 1) // BACK_SHARE[1]
                lax.fori_loop(*((0, middle) if part == 0 else (middle, tiles)), q_tile, 0)

    loop(sz.units, one)


def back_first_kernel(sz, first, count, recv_grad, qs, kvs, kept, dos, grad_q, grad_kv, key_t):
    dos[sz.tokens :, :] = jnp.zeros((Q_TILE, LANES), BF16)

    def unpack(src):
        at = pl.multiple_of(src * sz.slot, 16)
        unfold_into(dos, at, recv_grad[src], sz, True)
        grad_kv[pl.ds(at, sz.slot), :] = jnp.zeros((sz.slot, LANES), F32)

    loop(sz.n, unpack)
    back_tiles(sz, 0, first, count, qs, kvs, dos, kept, grad_q, grad_kv, key_t)


def back_last_kernel(
    sz, first, count, dos, qs, kvs, kept, grad_q_in, grad_kv_in, turns, out, grad_q, grad_kv, key_t
):
    def copy(src):
        rows = pl.ds(pl.multiple_of(src * sz.slot, 16), sz.slot)
        grad_q[rows, :] = grad_q_in[rows, :]
        grad_kv[rows, :] = grad_kv_in[rows, :]

    loop(sz.n, copy)
    back_tiles(sz, 1, first, count, qs, kvs, dos, kept, grad_q, grad_kv, key_t)

    def pack(src):
        rows = pl.ds(pl.multiple_of(src * sz.slot, 16), sz.slot)
        kv = grad_kv[rows, :]
        left = lane_index((1, LANES)) < HEAD_DIM
        real = lax.broadcasted_iota(jnp.int32, (sz.slot, 1), 0) < sz.rows
        both = jnp.where(left, grad_q[rows, :], swap_halves(kv))
        table = turns[rows, :]
        other = swap_halves(table)
        both = rotate_pair(both, jnp.where(left, table, other), jnp.where(left, other, table), True)
        out[src, 0 : sz.slot, :] = jnp.where(real, jnp.where(left, swap_halves(both), kv), 0.0).astype(BF16)
        out[src, sz.slot :, :] = fold_head(both[: sz.rows], sz, False).astype(BF16)

    loop(sz.n, pack)


def attend_back_first(sz, first, count, recv_grad, qs, kvs, kept):
    smem = pl.BlockSpec(memory_space=pltpu.SMEM)
    vmem = pl.BlockSpec(memory_space=pltpu.VMEM)
    shape = jax.ShapeDtypeStruct
    return pl.pallas_call(
        lambda *refs: back_first_kernel(sz, *refs),
        in_specs=[smem, smem] + [vmem] * 4,
        out_specs=[vmem] * 3,
        out_shape=[
            shape((sz.tokens + Q_TILE, LANES), BF16),
            shape((sz.tokens + Q_TILE, LANES), F32),
            shape((sz.tokens, LANES), F32),
        ],
        scratch_shapes=[pltpu.VMEM((HEAD_DIM, CLIP_MAX // CLIP_MIN * sz.unit_rows), BF16)],
        compiler_params=params(),
        cost_estimate=cost(40),
        name="attend_back_first",
    )(first, count, recv_grad, qs, kvs, kept)


def attend_back_last(sz, first, count, dos, qs, kvs, kept, grad_q, grad_kv, turns):
    smem = pl.BlockSpec(memory_space=pltpu.SMEM)
    vmem = pl.BlockSpec(memory_space=pltpu.VMEM)
    shape = jax.ShapeDtypeStruct
    return pl.pallas_call(
        lambda *refs: back_last_kernel(sz, *refs),
        in_specs=[smem, smem] + [vmem] * 7,
        out_specs=vmem,
        out_shape=shape((sz.n, sz.msg, LANES), BF16),
        scratch_shapes=[
            pltpu.VMEM((sz.tokens + Q_TILE, LANES), F32),
            pltpu.VMEM((sz.tokens, LANES), F32),
            pltpu.VMEM((HEAD_DIM, CLIP_MAX // CLIP_MIN * sz.unit_rows), BF16),
        ],
        compiler_params=params(),
        cost_estimate=cost(20),
        name="attend_back_last",
    )(first, count, dos, qs, kvs, kept, grad_q, grad_kv, turns)


def triple_grad_kernel(sz, grads, normed, out, total):
    step = pl.program_id(0)
    high = sz.slot - sz.fold
    part_kv = jnp.zeros((LANES, sz.width), F32)
    part_q = jnp.zeros((HEAD_DIM, sz.width), F32)
    sums = jnp.zeros((1, 2 * LANES), F32)
    for src in range(grads.shape[0]):
        key_value = grads[src, 0 : sz.slot, :]
        query = grads[src, sz.slot :, :]
        part_kv = part_kv + dot_rows(key_value, normed[src])
        part_q = part_q + dot_rows(query, normed[src, 0 : sz.fold, :])[:HEAD_DIM]
        part_q = part_q + dot_rows(query[:high], normed[src, sz.fold :, :])[HEAD_DIM:]
        sum_kv = jnp.sum(key_value.astype(F32), axis=0, keepdims=True)
        sum_q = jnp.sum(query.astype(F32), axis=0, keepdims=True)
        sums = sums + jnp.concatenate([sum_kv, sum_q + swap_halves(sum_q)], axis=1)

    @pl.when(step == 0)
    def _():
        total[...] = jnp.zeros_like(total)

    total[0:LANES, :] += part_kv
    total[LANES : LANES + HEAD_DIM, :] += part_q
    total[2 * LANES :, 0 : 2 * LANES] += jnp.broadcast_to(sums, (8, 2 * LANES))

    @pl.when(step == pl.num_programs(0) - 1)
    def _():
        few = sz.width // sz.shards
        bias = total[2 * LANES : 2 * LANES + 1, 0 : 2 * LANES]
        place = lax.broadcasted_iota(jnp.int32, (sz.width, 1), 0) % few
        left = lane_index((1, LANES)) < HEAD_DIM
        out[:, 0:LANES] = total[0:LANES, :].T
        queries = total[LANES : 2 * LANES, :].T
        kv_row, q_row = bias[:, 0:LANES], bias[:, LANES:]
        side = jnp.where(place == 0, swap_halves(kv_row), jnp.where(place == 1, kv_row, q_row))
        out[:, LANES:] = jnp.where(left, queries, side)


def triple_grad(sz, grads, normed_all):
    shape = jax.ShapeDtypeStruct
    last = sz.n // 2 - 1
    return pl.pallas_call(
        lambda *refs: triple_grad_kernel(sz, *refs),
        grid=(sz.n // 2,),
        in_specs=[
            pl.BlockSpec((2, sz.msg, LANES), lambda j: (j, 0, 0)),
            pl.BlockSpec((2, sz.slot, sz.width), lambda j: (jnp.where(j % 2 == 0, j // 2, last - j // 2), 0, 0)),
        ],
        out_specs=pl.BlockSpec((sz.width, 2 * LANES), lambda j: (0, 0)),
        out_shape=shape((sz.width, 2 * LANES), F32),
        scratch_shapes=[pltpu.VMEM((2 * LANES + 8, sz.width), F32)],
        compiler_params=params(),
        cost_estimate=cost(1),
        name="triple_grad",
    )(grads, normed_all)


def choose(pieces, index):
    picked = pieces[0]
    for at in range(1, len(pieces)):
        picked = jnp.where(index == at, pieces[at], picked)
    return picked


def core_cols(block, width, side):
    count = block.shape[1] // (2 * width)
    groups = [block[:, g * width : (g + 1) * width] for g in range(2 * count)]
    return jnp.concatenate([choose(groups[2 * g : 2 * g + 2], side) for g in range(count)], axis=1)


def feed_kernel(sz, place, tok, heads_in, wo, bo, gain, offset, we, be, wr, br, cot, *refs):
    result, grad_hidden, msg, shared, act_own, grad_be, grad_gain, grad_offset, grad_bo, grad_br = refs[:10]
    hidden, reduced, grad_normed = refs[10:]
    step = pl.program_id(0)
    core = place[0]
    left = lane_index((sz.fold, LANES)) < HEAD_DIM
    normed = shared.at[:, sz.ff : sz.ff + sz.width]
    attended = shared.at[:, sz.ff + sz.width : sz.ff + 2 * sz.width]

    @pl.when(step == 0)
    def _():
        for pair in range(sz.heads // 2):
            a = heads_in[2 * pair, 0 : sz.fold, :].astype(F32)
            b = heads_in[2 * pair + 1, 0 : sz.fold, :].astype(F32)
            low = jnp.where(left, a, swap_halves(b))
            high = jnp.where(left, swap_halves(a), b)[: sz.rest]
            both = jnp.concatenate([low, high], axis=0)
            attended[:, pair * LANES : (pair + 1) * LANES] = both.astype(BF16)
        rows = tok[...].astype(F32) + (dot(attended[...], wo[...]) + bo[...])
        hidden[...] = rows
        unit, _ = norm_parts(rows)
        normed[...] = (unit * gain[...] + offset[...]).astype(BF16)
        reduced[...] = jnp.zeros_like(reduced)
        grad_normed[...] = jnp.zeros_like(grad_normed)

    expanded = dot(normed[...], we[...]) + be[...]
    below = 0.5 * (1.0 + lax.erf(expanded * 0.7071067811865476))
    bell = jnp.exp(expanded * expanded * -0.5) * 0.3989422804014327
    activated = expanded * below
    slope = below + expanded * bell
    act_low = activated.astype(BF16)
    reduced[...] += dot(act_low, wr[...])
    grad_expanded = (dot_cols(cot[...], wr[...]) * slope).astype(BF16)
    grad_be[...] = jnp.sum(grad_expanded.astype(F32), axis=0, keepdims=True)
    grad_normed[...] += dot_cols(grad_expanded, we[...])
    span = act_low.shape[1]
    act_own[...] = core_cols(activated, sz.ff // sz.n, core).astype(BF16)
    sent_at = sz.ff + 3 * sz.width
    shared[:, pl.ds(pl.multiple_of(sent_at + step * (span // 2), LANES), span // 2)] = core_cols(
        activated, sz.ff // sz.n, 1 - core
    ).astype(BF16)
    shared[:, pl.ds(pl.multiple_of(step * span, LANES), span)] = grad_expanded

    @pl.when(step == pl.num_programs(0) - 1)
    def _():
        rows = hidden[...]
        out_grad = cot[...].astype(F32)
        result[...] = (rows + (reduced[...] + br[...])).astype(BF16)
        part, gain_part, offset_part = norm_back(grad_normed[...], rows, gain[...])
        total = out_grad + part
        grad_hidden[...] = total
        grad_gain[...] = gain_part
        grad_offset[...] = offset_part
        grad_br[...] = jnp.sum(out_grad, axis=0, keepdims=True)
        low = total.astype(BF16)
        shared[:, sz.ff + 2 * sz.width : sz.ff + 3 * sz.width] = low
        grad_bo[...] = jnp.sum(low.astype(F32), axis=0, keepdims=True)
        for quarter in range(4):
            wide = sz.width // 4
            grad_attended = dot_cols(low, wo[quarter * wide : (quarter + 1) * wide, :])
            for pair in range(wide // LANES):
                both = grad_attended[:, pair * LANES : (pair + 1) * LANES]
                head = 2 * (quarter * (wide // LANES) + pair)
                msg[head] = fold_head(both, sz, False).astype(BF16)
                msg[head + 1] = fold_head(both, sz, True).astype(BF16)


def feed(sz, place, tokens, heads_in, wo, bo, gain, offset, we, be, wr, br, cot):
    span = 512
    steps = sz.ff // span
    whole = lambda *shape: pl.BlockSpec(shape, lambda j: (0,) * len(shape))
    shape = jax.ShapeDtypeStruct
    vector = whole(1, sz.width)
    vector_out = shape((1, sz.width), F32)
    shared = sz.ff + 3 * sz.width + sz.ff // 2
    return pl.pallas_call(
        lambda *refs: feed_kernel(sz, *refs),
        grid=(steps,),
        in_specs=[
            pl.BlockSpec(memory_space=pltpu.SMEM),
            whole(sz.rows, sz.width),
            whole(sz.heads, sz.fold, LANES),
            whole(sz.width, sz.width),
            vector,
            vector,
            vector,
            pl.BlockSpec((sz.width, span), lambda j: (0, j)),
            pl.BlockSpec((1, span), lambda j: (0, j)),
            pl.BlockSpec((span, sz.width), lambda j: (j, 0)),
            vector,
            whole(sz.rows, sz.width),
        ],
        out_specs=[
            whole(sz.rows, sz.width),
            whole(sz.rows, sz.width),
            whole(sz.heads, sz.fold, LANES),
            whole(sz.rows, shared),
            pl.BlockSpec((sz.rows, span // 2), lambda j: (0, j)),
            pl.BlockSpec((1, span), lambda j: (0, j)),
            vector,
            vector,
            vector,
            vector,
        ],
        out_shape=[
            shape((sz.rows, sz.width), BF16),
            shape((sz.rows, sz.width), F32),
            shape((sz.heads, sz.fold, LANES), BF16),
            shape((sz.rows, shared), BF16),
            shape((sz.rows, sz.ff // 2), BF16),
            shape((1, sz.ff), F32),
            vector_out,
            vector_out,
            vector_out,
            vector_out,
        ],
        scratch_shapes=[pltpu.VMEM((sz.rows, sz.width), F32)] * 3,
        compiler_params=params(),
        cost_estimate=cost(28),
        name="feed",
    )(place, tokens, heads_in, wo, bo, gain, offset, we, be, wr, br, cot)


def weights_kernel(sz, place, act, act_got, cot, cot_got, back, back_got, norm, norm_got, *refs):
    att, att_got, low, low_got = refs[:4]
    wr_own, wr_sent, wo_own, wo_sent = refs[4:8]
    we_out = refs[8 : 8 + sz.m]
    norm_t, norm_t_got = refs[8 + sz.m :]
    step = pl.program_id(0)
    core, low_bit, next_bit, mine_dp = place[0], place[1], place[2], place[3]
    per = sz.width // sz.n

    def core_rows(block):
        turned = block[...].astype(F32).T.reshape(sz.n // 2, 2, per, sz.rows)
        return choose([turned[:, 0], turned[:, 1]], core).reshape(sz.width // 2, sz.rows).astype(BF16)

    @pl.when(step == 0)
    def _():
        norm_t[...] = core_rows(norm)
        norm_t_got[...] = core_rows(norm_got)
        grad_wo = dot(core_rows(att), low[...]) + dot(core_rows(att_got), low_got[...])
        grad_wo = grad_wo.reshape(sz.n // 8, 2, 2 * per, sz.width)
        sides = [grad_wo[:, 0], grad_wo[:, 1]]
        wo_own[...] = choose(sides, next_bit).astype(BF16)
        wo_sent[...] = choose(sides, 1 - next_bit).astype(BF16)

    groups = act.shape[1] // (sz.ff // sz.n)
    grad_wr = (dot_rows(act[...], cot[...]) + dot_rows(act_got[...], cot_got[...])).astype(BF16)
    grad_wr = grad_wr.reshape(groups, sz.ff // sz.n, sz.width)
    if groups == 1:

        @pl.when(step % 2 == low_bit)
        def _():
            wr_own[...] = grad_wr

        @pl.when(step % 2 != low_bit)
        def _():
            wr_sent[...] = grad_wr

    else:
        wr_own[...] = choose([grad_wr[0:1], grad_wr[1:2]], low_bit)
        wr_sent[...] = choose([grad_wr[0:1], grad_wr[1:2]], 1 - low_bit)
    grad_we = dot(norm_t[...], back[...]) + dot(norm_t_got[...], back_got[...])
    grad_we = grad_we.reshape(sz.n // 2, sz.m, per // sz.m, grad_we.shape[1])
    sides = [grad_we[:, q] for q in range(sz.m)]
    for by in range(sz.m):
        piece = choose(sides, lax.rem(mine_dp + by, sz.m))
        we_out[by][...] = piece.astype(BF16).reshape(we_out[by].shape)


def weights(sz, place, act, cot, cot_got, shared, shared_got):
    span = 512
    steps = sz.ff // span
    per = sz.width // span
    fan = sz.ff // sz.width
    half = sz.n // 2
    few = sz.width // sz.shards
    whole = lambda *shape: pl.BlockSpec(shape, lambda j: (0,) * len(shape))
    column = lambda k: pl.BlockSpec((sz.rows, sz.width), lambda j: (0, sz.ff // sz.width + k))
    block = pl.BlockSpec((sz.rows, span), lambda j: (0, j))
    act_block = pl.BlockSpec((sz.rows, span // 2), lambda j: (0, j))
    got_at = (sz.ff + 3 * sz.width) // (span // 2)
    got_block = pl.BlockSpec((sz.rows, span // 2), lambda j: (0, got_at + j))
    shape = jax.ShapeDtypeStruct
    groups = half // steps
    wr_block = pl.BlockSpec((1, sz.ff // sz.n, sz.width), lambda j: (j * groups // 2, 0, 0))
    wr_out = shape((half // 2, sz.ff // sz.n, sz.width), BF16)
    wo_dims = (sz.n // 8, 2 * sz.width // sz.n, sz.width)
    we_block = pl.BlockSpec((half, 1, few, span), lambda j: (0, j // per, 0, j % per))
    we_out = shape((half, fan, few, sz.width), BF16)
    return pl.pallas_call(
        lambda *refs: weights_kernel(sz, *refs),
        grid=(steps,),
        in_specs=[
            pl.BlockSpec(memory_space=pltpu.SMEM),
            act_block,
            got_block,
            whole(sz.rows, sz.width),
            whole(sz.rows, sz.width),
            block,
            block,
        ]
        + [column(k // 2) for k in range(6)],
        out_specs=[wr_block, wr_block, whole(*wo_dims), whole(*wo_dims)] + [we_block] * sz.m,
        out_shape=[wr_out, wr_out, shape(wo_dims, BF16), shape(wo_dims, BF16)] + [we_out] * sz.m,
        scratch_shapes=[pltpu.VMEM((sz.width // 2, sz.rows), BF16)] * 2,
        compiler_params=params(),
        cost_estimate=cost(10),
        name="weights",
    )(place, act, shared_got, cot, cot_got, shared, shared_got, *([shared, shared_got] * 3))


def finish_kernel(sz, back, wq, wk, wv, tok, gain, grad_hidden, input_grad, grad_normed):
    step = pl.program_id(0)
    left = lane_index((sz.rows, LANES)) < HEAD_DIM
    left_fold = lane_index((sz.fold, LANES)) < HEAD_DIM
    queries, keys, values = [], [], []
    for pair in range(wq.shape[1] // LANES):
        kv_a = back[2 * pair, 0 : sz.rows, :].astype(F32)
        kv_b = back[2 * pair + 1, 0 : sz.rows, :].astype(F32)
        q_a = back[2 * pair, sz.slot : sz.slot + sz.fold, :].astype(F32)
        q_b = back[2 * pair + 1, sz.slot : sz.slot + sz.fold, :].astype(F32)
        low = jnp.where(left_fold, q_a, swap_halves(q_b))
        high = jnp.where(left_fold, swap_halves(q_a), q_b)[: sz.rest]
        queries.append(jnp.concatenate([low, high], axis=0).astype(BF16))
        keys.append(jnp.where(left, kv_a, swap_halves(kv_b)).astype(BF16))
        values.append(jnp.where(left, swap_halves(kv_a), kv_b).astype(BF16))
    total = jnp.zeros((sz.rows, sz.width), F32)
    for parts, weight in ((queries, wq), (keys, wk), (values, wv)):
        total = total + dot_cols(jnp.concatenate(parts, axis=1), weight[...])

    @pl.when(step == 0)
    def _():
        grad_normed[...] = total

    @pl.when(step > 0)
    def _():
        grad_normed[...] += total

    @pl.when(step == pl.num_programs(0) - 1)
    def _():
        part, _, _ = norm_back(grad_normed[...], tok[...].astype(F32), gain[...])
        input_grad[...] = grad_hidden[...] + part


def finish(sz, back, weight, tokens, gain, grad_hidden):
    cols = 256
    steps = sz.width // cols
    whole = lambda *shape: pl.BlockSpec(shape, lambda j: (0,) * len(shape))
    part = lambda k: pl.BlockSpec((sz.width, cols), lambda j: (0, k * steps + j))
    return pl.pallas_call(
        lambda *refs: finish_kernel(sz, *refs),
        grid=(steps,),
        in_specs=[
            pl.BlockSpec((cols // HEAD_DIM, sz.msg, LANES), lambda j: (j, 0, 0)),
            part(0),
            part(1),
            part(2),
            whole(sz.rows, sz.width),
            whole(1, sz.width),
            whole(sz.rows, sz.width),
        ],
        out_specs=whole(sz.rows, sz.width),
        out_shape=jax.ShapeDtypeStruct((sz.rows, sz.width), F32),
        scratch_shapes=[pltpu.VMEM((sz.rows, sz.width), F32)],
        compiler_params=params(),
        cost_estimate=cost(10),
        name="finish",
    )(back, weight, weight, weight, tokens, gain, grad_hidden)


def pick(array, axis, index):
    return lax.dynamic_index_in_dim(array, index, axis, keepdims=False)


def after(value, *others):
    return lax.optimization_barrier((value,) + others)[0]


class Halving:
    def __init__(self, sz, value, labels):
        self.sz = sz
        self.labels = list(labels)
        self.parts = [value]

    def picked(self, axis, index):
        return sum(pick(part, axis, index).astype(F32) for part in self.parts)

    def send(self, label):
        sz = self.sz
        axis = self.labels.index(label)
        self.labels.remove(label)
        if label == "dp":
            mine = lax.axis_index("dp")
            outs = [self.picked(axis, (mine + by) % sz.m).astype(BF16) for by in range(1, sz.m)]
        else:
            mine = (lax.axis_index("seq") // (2 << label)) % 2
            outs = [self.picked(axis, 1 - mine).astype(BF16)]
        self.parts = [self.picked(axis, mine)]
        return outs

    def move(self, label, outs):
        sz = self.sz
        if label == "dp":
            return [
                lax.ppermute(block, "dp", [(i, (i + by + 1) % sz.m) for i in range(sz.m)])
                for by, block in enumerate(outs)
            ]
        bit = 2 << label
        return [lax.ppermute(block, "seq", [(i, i ^ bit) for i in range(sz.n)]) for block in outs]

    def add(self, got):
        self.parts = self.parts + list(got)

    def value(self):
        return sum(part.astype(F32) for part in self.parts)

    def stage(self, label):
        self.add(self.move(label, self.send(label)))


def per_device(
    tokens,
    clip_start,
    frames,
    positions,
    first_gain,
    first_offset,
    triple_weight,
    triple_bias,
    output_weight,
    output_bias,
    second_gain,
    second_offset,
    expand_weight,
    expand_bias,
    reduce_weight,
    reduce_bias,
    cotangent,
):
    rows, width = tokens.shape[1:]
    ff = expand_weight.shape[1]
    n = lax.axis_size("seq")
    m = lax.axis_size("dp")
    slabs = clip_start.shape[1]
    sz = Sizes(rows, width, ff, n, m, slabs)
    shards = n * m
    group_slabs = n * slabs
    lower, upper = slab_bounds(clip_start[0], frames[0], lax.axis_index("seq") * slabs, group_slabs)
    first_unit = lower[0] // CLIP_MIN
    unit_count = (upper[0] - lower[0]) // CLIP_MIN
    meta_rows = jnp.arange(8)[:, None]
    meta = jnp.where(meta_rows == 0, first_unit, jnp.where(meta_rows == 1, unit_count, 0))
    meta = jnp.where(jnp.arange(LANES) < HEAD_DIM, 0, meta).astype(F32)
    cos, sin = lane_tables(positions[0])
    row = lambda vector: vector.reshape(1, -1)
    me, mine_dp = lax.axis_index("seq"), lax.axis_index("dp")
    place = jnp.stack([me % 2, me // 2 % 2, me // 4 % 2, mine_dp])
    swap_core = lambda block: lax.ppermute(block, "seq", [(i, i ^ 1) for i in range(n)])

    def exchange(message):
        if sz.rep > 1:
            message = jnp.repeat(message, sz.rep, axis=0)
        return lax.all_to_all(message, "seq", 0, 0, tiled=True)

    cot_got = swap_core(cotangent[0])
    message, normed = project(
        sz, tokens[0], row(first_gain), row(first_offset), triple_weight, row(triple_bias), cos, sin, meta
    )
    recv = exchange(message)
    places = jnp.pad(positions[0].astype(BF16), ((0, sz.slot - rows - 3), (0, width - rows)))
    normed_all = jnp.concatenate([normed, places], axis=0)
    chips = list(range(0, n // 2, 2)) + list(range(n // 2 - 1, 0, -2))
    ring = [2 * chip + core for chip in chips for core in range(2)]
    normed_all = lax.all_gather(after(normed_all, recv), "seq", axis=0, tiled=False, axis_index_groups=[ring])
    back_order = [ring.index(src) for src in range(n)]
    turns = all_turns(normed_all[:, rows : rows + 3, :rows][jnp.array(back_order)])
    facts = recv[:: sz.per_unit, sz.msg - 8 : sz.msg - 6, LANES - 1].astype(jnp.int32)
    unit_first, unit_span = facts[:, 0], facts[:, 1]
    out_message, kept, qs, kvs = attend(sz, unit_first, unit_span, recv)
    heads_in = lax.all_to_all(out_message, "seq", 0, 0, tiled=True)[:: sz.rep]
    (
        result,
        grad_hidden,
        grad_message,
        shared,
        act_own,
        grad_be,
        grad_second_gain,
        grad_second_offset,
        grad_bo,
        grad_br,
    ) = feed(
        sz,
        place,
        tokens[0],
        heads_in,
        output_weight,
        row(output_bias),
        row(second_gain),
        row(second_offset),
        expand_weight,
        row(expand_bias),
        reduce_weight,
        row(reduce_bias),
        cotangent[0],
    )
    recv_grad = exchange(grad_message)
    half = n // 2
    fan = ff // width
    few = width // shards
    many = ff // shards
    columns = [
        grad_bo.reshape(width, 1),
        grad_second_gain.reshape(width, 1),
        grad_second_offset.reshape(width, 1),
        grad_be.reshape(width, fan),
        grad_br.reshape(width, 1),
    ]
    small = jnp.concatenate(columns, axis=1)
    shared_got = swap_core(shared)
    wr_own, wr_sent, wo_own, wo_sent, *we_parts = weights(
        sz, place, act_own, cotangent[0], cot_got, shared, shared_got
    )
    bits = list(range(half.bit_length() - 2, -1, -1))
    twos = lambda count: (2,) * count
    wr_shape = twos(len(bits) - 1) + (m, many, width)
    we_shape = twos(len(bits)) + (many, width)
    wo_shape = twos(len(bits) - 1) + (m, few, width)
    side_r = Halving(sz, wr_own.reshape(wr_shape), bits[:-1] + ["dp"])
    side_e = Halving(sz, we_parts[0].reshape(we_shape), bits)
    side_o = Halving(sz, wo_own.reshape(wo_shape), bits[:-2] + [0, "dp"])
    small = small.reshape(twos(len(bits)) + (2, m, -1))
    small_got = swap_core(pick(small, len(bits), 1 - me % 2))
    side_s = Halving(sz, pick(small, len(bits), me % 2), bits + ["dp"])
    side_s.add([small_got])
    recv_grad = after(recv_grad, wr_sent, turns)
    got_r = side_r.move(0, [wr_sent.reshape(wr_shape)])
    got_e = side_e.move("dp", [part.reshape(we_shape) for part in we_parts[1:]])
    got_o = side_o.move(1, [wo_sent.reshape(wo_shape)])
    out_s = side_s.send(1)
    got_s = side_s.move(1, out_s)
    dos, grad_q, grad_kv = attend_back_first(sz, unit_first, unit_span, recv_grad, qs, kvs, kept)
    side_r.add(after(got_r, grad_kv))
    side_e.add(after(got_e, grad_kv))
    side_o.add(after(got_o, grad_kv))
    side_s.add(after(got_s, grad_kv))
    small_sum = side_s.value()
    small_sum = jnp.pad(
        small_sum[..., None, :], [(0, 0)] * small_sum.ndim + [(0, width - small_sum.shape[-1])]
    )
    small_sum = jnp.pad(small_sum, [(0, 0)] * (small_sum.ndim - 2) + [(0, 7), (0, 0)])
    side_o.parts = [jnp.concatenate([side_o.value(), small_sum], axis=-2)]
    out_r, out_e, out_o = side_r.send("dp"), side_e.send(0), side_o.send("dp")
    got_r, got_e, got_o = side_r.move("dp", out_r), side_e.move(0, out_e), side_o.move("dp", out_o)
    back_message = attend_back_last(
        sz, unit_first, unit_span, after(dos, out_r, out_e, out_o), qs, kvs, kept, grad_q, grad_kv, turns
    )
    got_r, got_e, got_o = after((got_r, got_e, got_o), back_message)
    side_r.add(got_r)
    side_e.add(got_e)
    side_o.add(got_o)
    out_r, out_e, out_o = side_r.send(1), side_e.send(1), side_o.send(0)
    got_r, got_e, got_o = side_r.move(1, out_r), side_e.move(1, out_e), side_o.move(0, out_o)
    back = lax.all_to_all(after(back_message, out_r, out_e, out_o), "seq", 0, 0, tiled=True)[:: sz.rep]
    head_grad = triple_grad(sz, after(back_message, out_r, out_e, out_o), normed_all)
    side_r.add(after(got_r, head_grad))
    side_e.add(after(got_e, head_grad))
    side_o.add(after(got_o, head_grad))
    out_r, out_e, out_o = side_r.send(2), side_e.send(2), side_o.send(2)
    got_r, got_e, got_o = side_r.move(2, out_r), side_e.move(2, out_e), side_o.move(2, out_o)
    input_grad = finish(sz, back, triple_weight, tokens[0], row(first_gain), grad_hidden)
    side_r.add(after(got_r, input_grad))
    side_e.add(after(got_e, input_grad))
    side_o.add(after(got_o, input_grad))
    for bit in range(3, len(bits)):
        side_r.stage(bit)
        side_e.stage(bit)
        side_o.stage(bit)
    head_parts = head_grad.reshape(n, m, few, 2 * LANES)
    head_sum = pick(head_parts, 1, mine_dp)
    for by in range(1, m):
        block = pick(head_parts, 1, (mine_dp + by) % m)
        head_sum = head_sum + lax.ppermute(block, "dp", [(i, (i + by) % m) for i in range(m)])
    head_rows = lax.all_to_all(after(head_sum, back), "seq", 0, 0, tiled=True)[:: sz.rep]
    parts = [head_rows[:, :, k * HEAD_DIM : (k + 1) * HEAD_DIM] for k in (2, 0, 1)]
    out_wt = jnp.concatenate([part.transpose(1, 0, 2).reshape(few, width) for part in parts], axis=1)
    bias_all = jnp.concatenate([head_rows[:, k, 3 * HEAD_DIM :].reshape(width) for k in (2, 0, 1)])
    shard = lax.axis_index("seq") * m + mine_dp
    bias_qk = lax.dynamic_slice(bias_all, (shard * 2 * few,), (2 * few,))
    bias_v = lax.dynamic_slice(bias_all, (2 * width + shard * few,), (few,))
    weight_rows = lax.dynamic_slice(triple_weight, (shard * few, 0), (few, 3 * width)).astype(F32)
    gain_rows = lax.dynamic_slice(first_gain, (shard * few,), (few,))
    offset_rows = lax.dynamic_slice(first_offset, (shard * few,), (few,))
    offset_one = jnp.sum(weight_rows * bias_all, axis=1)
    gain_one = (jnp.sum(weight_rows * out_wt, axis=1) - offset_rows * offset_one) / gain_rows
    out_wr = side_r.value()
    out_we = side_e.value().reshape(fan, few, width).transpose(1, 0, 2).reshape(few, ff)
    last_o = side_o.value()
    out_wo = last_o[:few]
    vectors = last_o[few, : small.shape[-1]].reshape(few, -1)
    begin = 0
    outs = []
    for column in columns:
        wide = column.shape[1]
        outs.append(vectors[:, begin : begin + wide].reshape(-1))
        begin += wide
    bias_o, gain_two, offset_two, bias_e, bias_r = outs
    return (
        result[None],
        input_grad[None],
        gain_one,
        offset_one,
        out_wt,
        bias_qk,
        bias_v,
        out_wo,
        bias_o,
        gain_two,
        offset_two,
        out_we,
        bias_e,
        out_wr,
        bias_r,
    )


def solution(mesh):
    sharded = P("dp", "seq", None)
    placed = (
        (sharded, P("dp", "seq"), P("dp", "seq"), P("dp", None, "seq"))
        + (P(),) * 12
        + (sharded,)
    )
    vector = P(("seq", "dp"))
    matrix = P(("seq", "dp"), None)
    return jax.shard_map(
        per_device,
        mesh=mesh,
        in_specs=placed,
        out_specs=(sharded, sharded, vector, vector, matrix, vector, vector, matrix, vector)
        + (vector, vector, matrix, vector, matrix, vector),
        check_vma=False,
    )
```

time: 2630 us -> 445 us (0.17)
  waiting for transfers between devices: 969 us -> 129 us
  starting transfers between devices: 708 us -> 50.2 us
  local copies, waits for them, and re-layouts: 413 us -> 28.3 us
  matrix products: 200 us -> 4.52 us
  Pallas kernels: 0 us -> 176 us
  blocking collectives: 124 us -> 0 us
  other arithmetic: 119 us -> 36.9 us
  loops' own time: 60.8 us -> 0 us
    reduce_scatter x4 -> x0, waiting for transfers between devices: 781 us -> none  [the longest x1 361 us: per_device(): lax.psum_scatter(grad_reduce_weight, ('seq', 'dp'), scatter_dimension=0,...]
    ppermute x28 -> x17, starting transfers between devices: 707 us -> 15.4 us  [the longest x10 12.1 us: move(): lax.ppermute(block, 'seq', [(i, i ^ bit) for i in range(sz.n)])]
    dot_general x30 -> x1, matrix products: 200 us -> 4.52 us  [all_turns(): return jnp.dot(hit, table, precision=lax.Precision.HIGHEST)]
    pallas_call x0 -> x8, Pallas kernels: none -> 176 us  [the longest x1 43.5 us: attend_back_first(): pl.pallas_call(lambda *refs: back_first_kernel(sz, *refs), in_specs=[smem...]
    ppermute x28 -> x17, waiting for transfers between devices: 188 us -> 49.3 us  [the longest x10 49.3 us: move(): lax.ppermute(block, 'seq', [(i, i ^ bit) for i in range(sz.n)])]
    dynamic_update_slice x30 -> x0, local copies, waits for them, and re-layouts: 138 us -> none  [per_device(): lax.scan(back_step, zero_heads, (stacked, shift_table))]
    unnamed x1 -> x0, blocking collectives: 124 us -> none
    all_to_all x0 -> x5, waiting for transfers between devices: none -> 79.8 us  [the longest x2 46.9 us: exchange(): return lax.all_to_all(message, 'seq', 0, 0, tiled=True)]
  transfers between devices with their start and end apart: 32 -> 23, of which waited for: 11 -> 5; matrix products, arithmetic and copies ran while one was open for 18% -> 10% of each run, Pallas kernels for 0% -> 38%
where the time goes in v1:
time: 445 us; the launch traced here: 441 us
  Pallas kernels  176 us (40%)
  waiting for transfers between devices  129 us (29%)
  starting transfers between devices  50.2 us (11%)
  other arithmetic  36.9 us (8%)
  local copies, waits for them, and re-layouts  28.3 us (6%)
  between operations  15.2 us (3%)
  matrix products  4.52 us (1%)
    ppermute x10, waiting for transfers between devices, move(): lax.ppermute(block, 'seq', [(i, i ^ bit) for i in range(sz.n)])  49.3 us
    all_to_all x2, waiting for transfers between devices, exchange(): return lax.all_to_all(message, 'seq', 0, 0, tiled=True)  46.9 us
    pallas_call x1, Pallas kernels, attend_back_first(): pl.pallas_call(lambda *refs: back_first_kernel(sz, *refs), in_specs=[smem...  43.5 us
    all_to_all x1, waiting for transfers between devices, per_device(): heads_in = lax.all_to_all(out_message, 'seq', 0, 0, tiled=True)[::sz.rep]  32.9 us
    pallas_call x1, Pallas kernels, attend(): pl.pallas_call(lambda *refs: attend_kernel(sz, *refs), in_specs=[smem, sm...  28.5 us
    pallas_call x1, Pallas kernels, feed(): pl.pallas_call(lambda *refs: feed_kernel(sz, *refs), grid=(steps,), in_sp...  28.1 us
    pallas_call x1, Pallas kernels, attend_back_last(): pl.pallas_call(lambda *refs: back_last_kernel(sz, *refs), in_specs=[smem,...  26.2 us
    pallas_call x1, Pallas kernels, weights(): pl.pallas_call(lambda *refs: weights_kernel(sz, *refs), grid=(steps,), in...  19.2 us
  transfers between devices with their start and end apart: 23, of which 5 were waited for; matrix products, arithmetic and copies ran while one was open for 10% of the time, Pallas kernels for 38%

profile of v1, /device:TPU:0, one launch (start us, length us, event | category | flops | bytes accessed | tf_op | source)
XLA Modules:
  0.0 440.6 jit_solution(14491323805525590636)
XLA Ops:
  10.0 1.6 fusion.16
  11.6 9.4 %project.1 = (bf16[16,608,128]{2,1,0:T(8,128)(2,1)}, bf16[392,1024]{1,0:T(8,128)(2,1)}) custom-call(bf16[392,1024]{1,0:T(8,128)(2,1)} %bitcast.238, f32[1,1024]{1,0:T(1,128)} %bitcast.234, f32[1,1024]{1,0:T(1,128)} %bitcast.236, bf16[1024,3072]{1,0:T(8,128)(2,1)} %refs_3_.5, bf16[1024,3072]{1,0:T(8,128)(2,1)} %refs_3_.5, bf16[1024,3072]{1,0:T(8,128)(2,1)} %refs_3_.5, ...), custom_call_target="tpu_custom_call" | custom-call | flops 9200000000 | bytes 1048576 | tf_op jit(solution)/shard_map/project/pallas_call | solution.py:201
  21.0 7.5 %all-to-all-start = ((bf16[16,608,128]{2,1,0:T(8,128)(2,1)}), bf16[16,608,128]{2,1,0:T(8,128)(2,1)S(1)}, u32[]{:S(2)}, u32[]{:S(2)}) async-start(bf16[16,608,128]{2,1,0:T(8,128)(2,1)} %get-tuple-element.274), calls=%async_computation | async-start | bytes 4980736 | tf_op jit(solution)/shard_map/all_to_all | solution.py:875
  28.6 1.0 fusion.5
  29.6 46.9 %all-to-all-done.refs_2_ = bf16[16,608,128]{2,1,0:T(8,128)(2,1)S(1)} async-done(((bf16[16,608,128]{2,1,0:T(8,128)(2,1)}), bf16[16,608,128]{2,1,0:T(8,128)(2,1)S(1)}, u32[]{:S(2)}, u32[]{:S(2)}) %all-to-all-start) | async-done | bytes 2490400 | tf_op jit(solution)/shard_map/all_to_all | solution.py:875
  76.5 1.5 copy-done.8
  78.7 28.5 %attend.1 = (bf16[16,208,128]{2,1,0:T(8,128)(2,1)}, f32[6656,128]{1,0:T(8,128)}, bf16[6656,128]{1,0:T(8,128)(2,1)}, bf16[6400,128]{1,0:T(8,128)(2,1)}) custom-call(s32[8]{0:T(128)} %get-tuple-element.359.refs_0_, s32[8]{0:T(128)} %get-tuple-element.358.refs_1_, bf16[16,608,128]{2,1,0:T(8,128)(2,1)} %copy-done.8), custom_call_target="tpu_custom_call" | custom-call | flops 36800000000 | bytes 1048576 | tf_op jit(solution)/shard_map/attend/pallas_call | solution.py:305
  107.2 12.8 %all-to-all-start.1 = ((bf16[16,208,128]{2,1,0:T(8,128)(2,1)}), bf16[16,208,128]{2,1,0:T(8,128)(2,1)S(1)}, u32[]{:S(2)}, u32[]{:S(2)}) async-start(bf16[16,208,128]{2,1,0:T(8,128)(2,1)} %get-tuple-element.275), calls=%async_computation.1 | async-start | bytes 1703936 | tf_op jit(solution)/shard_map/all_to_all | solution.py:892
  120.6 32.9 %all-to-all-done.1.refs_2_ = bf16[16,208,128]{2,1,0:T(8,128)(2,1)S(1)} async-done(((bf16[16,208,128]{2,1,0:T(8,128)(2,1)}), bf16[16,208,128]{2,1,0:T(8,128)(2,1)S(1)}, u32[]{:S(2)}, u32[]{:S(2)}) %all-to-all-start.1) | async-done | bytes 852000 | tf_op jit(solution)/shard_map/all_to_all | solution.py:892
  154.4 28.1 %feed.1 = (bf16[392,1024]{1,0:T(8,128)(2,1)}, f32[392,1024]{1,0:T(8,128)}, bf16[16,208,128]{2,1,0:T(8,128)(2,1)}, bf16[392,9216]{1,0:T(8,128)(2,1)}, bf16[392,20...) custom-call(s32[4]{0:T(128)} %pad_add_fusion.refs_0_, ...), custom_call_target="tpu_custom_call" | custom-call | flops 32199999488 | bytes 1048576 | tf_op jit(solution)/shard_map/feed/pallas_call | solution.py:587
  186.8 1.4 reduce.57
  190.5 3.6 all-to-all-start.2
  194.2 1.9 collective-permute-start.6
  196.1 19.2 %weights.1 = (bf16[4,256,1024]{2,1,0:T(8,128)(2,1)}, bf16[4,256,1024]{2,1,0:T(8,128)(2,1)}, bf16[2,128,1024]{2,1,0:T(8,128)(2,1)}, bf16[2,128,1024]{2,1,0:T(8,12...) custom-call(s32[4]{0:T(128)} %pad_add_fusion.refs_0_, ...), custom_call_target="tpu_custom_call" | custom-call | flops 11500000256 | bytes 1048576 | tf_op jit(solution)/shard_map/weights/pallas_call | solution.py:702
  215.3 3.2 copy.121
  218.6 1.5 collective-permute-start.2
  221.7 1.5 constant_dynamic-slice_fusion
  225.5 1.1 reshape.622
  226.6 4.5 %fusion.19.refs_8_ = f32[6400,128]{1,0:T(8,128)} fusion(pred[6400,48]{0,1:T(8,128)(4,1)S(1)} %reshape.622, f32[16,128]{1,0:T(8,128)S(1)} %get-tuple-element.348, f32[16,128]{1,0:T(8,128)S(1)} %get-tuple-element.347, f32[16,128]{1,0:T(8,128)S(1)} %get-tuple-element.346), kind=kOutput, calls=%fused_computation.53 | convolution fusion | flops 471871488 | bytes 3608576 | tf_op jit(solution)/shard_map/dot_general | solution.py:95
  232.0 43.5 %attend_back_first.1 = (bf16[6656,128]{1,0:T(8,128)(2,1)}, f32[6656,128]{1,0:T(8,128)}, f32[6400,128]{1,0:T(8,128)}) custom-call(s32[8]{0:T(128)} %get-tuple-element.359.refs_0_, s32[8]{0:T(128)} %get-tuple-element.358.refs_1_, bf16[16,208,128]{2,1,0:T(8,128)(2,1)} %copy-done.12, bf16[6656,128]{1,0:T(8,128)(2,1)} %get-tuple-element.284.refs_3_, ...), custom_call_target="tpu_custom_call" | custom-call | flops 46000001024 | bytes 1048576 | tf_op jit(solution)/shard_map/attend_back_first/pallas_call | solution.py:407
  275.6 1.5 copy_add_fusion
  277.3 1.0 copy-done.6
  278.4 4.3 convert_add_fusion.1
  282.7 4.2 convert_add_fusion
  287.1 2.0 collective-permute-start.9
  289.1 26.2 %attend_back_last.1.refs_0_ = bf16[16,608,128]{2,1,0:T(8,128)(2,1)} custom-call(s32[8]{0:T(128)} %get-tuple-element.359.refs_0_, s32[8]{0:T(128)} %get-tuple-element.358.refs_1_, bf16[6656,128]{1,0:T(8,128)(2,1)} %get-tuple-element.303.refs_2_, bf16[6656,128]{1,0:T(8,128)(2,1)} %get-tuple-element.284.refs_3_, bf16[6400,128]{1,0:T(8,128)(2,1)} %get-tuple-element.285.refs_4_, ...), custom_call_target="tpu_custom_call" | custom-call | flops 23000000512 | bytes 1048576 | tf_op jit(solution)/shard_map/attend_back_last/pallas_call | solution.py:427
  316.1 3.4 bitcast_add_fusion
  319.4 2.8 bitcast_add_fusion.1
  323.0 6.0 %all-to-all-start.3 = ((bf16[16,608,128]{2,1,0:T(8,128)(2,1)}), bf16[16,608,128]{2,1,0:T(8,128)(2,1)}, u32[]{:S(2)}, u32[]{:S(2)}) async-start(bf16[16,608,128]{2,1,0:T(8,128)(2,1)} %attend_back_last.1.refs_0_), calls=%async_computation.3 | async-start | bytes 4980736 | tf_op jit(solution)/shard_map/all_to_all | solution.py:976
  329.0 1.9 collective-permute-start.13
  331.1 12.1 %triple_grad.1 = f32[1024,256]{1,0:T(8,128)} custom-call(bf16[16,608,128]{2,1,0:T(8,128)(2,1)} %attend_back_last.1.refs_0_, bf16[16,400,1024]{2,1,0:T(8,128)(2,1)} %bitcast.206), custom_call_target="tpu_custom_call" | custom-call | flops 1150000000 | bytes 1048576 | tf_op jit(solution)/shard_map/triple_grad/pallas_call | solution.py:483
  343.2 2.0 dynamic-slice_bitcast_fusion
  345.5 1.8 collective-permute-start.11
  347.3 8.3 %collective-permute-done.11 = bf16[2,40,1024]{2,1,0:T(8,128)(2,1)S(1)} collective-permute-done((bf16[2,40,1024]{2,1,0:T(8,128)(2,1)}, bf16[2,40,1024]{2,1,0:T(8,128)(2,1)S(1)}, u32[]{:S(2)}, u32[]{:S(2)}) %collective-permute-start.11) | collective-permute-done | bytes 163872 | tf_op jit(solution)/shard_map/ppermute | solution.py:821
  355.7 1.0 collective-permute-start.12
  356.7 27.3 %collective-permute-done.13 = bf16[2,128,1024]{2,1,0:T(8,128)(2,1)} collective-permute-done((bf16[2,128,1024]{2,1,0:T(8,128)(2,1)}, bf16[2,128,1024]{2,1,0:T(8,128)(2,1)}, u32[]{:S(2)}, u32[]{:S(2)}) %collective-permute-start.13) | collective-permute-done | bytes 524320 | tf_op jit(solution)/shard_map/ppermute | solution.py:821
  384.0 1.9 fusion.14
  385.8 2.6 collective-permute-start.14
  388.4 13.7 %collective-permute-done.15 = bf16[2,128,1024]{2,1,0:T(8,128)(2,1)} collective-permute-done((bf16[2,128,1024]{2,1,0:T(8,128)(2,1)S(1)}, bf16[2,128,1024]{2,1,0:T(8,128)(2,1)}, u32[]{:S(2)}, u32[]{:S(2)}) %collective-permute-start.15) | collective-permute-done | bytes 524320 | tf_op jit(solution)/shard_map/ppermute | solution.py:821
  402.1 1.7 fusion.15
  404.3 1.9 bitcast_add_fusion.4
  406.2 4.9 %all-to-all-start.4 = ((f32[16,32,256]{2,1,0:T(8,128)}), f32[16,32,256]{2,1,0:T(8,128)S(1)}, u32[]{:S(2)}, u32[]{:S(2)}) async-start(f32[16,32,256]{2,1,0:T(8,128)} %bitcast_add_fusion.4), calls=%async_computation.4 | async-start | bytes 1048576 | tf_op jit(solution)/shard_map/all_to_all | solution.py:996
  411.1 9.4 %finish.1 = f32[392,1024]{1,0:T(8,128)} custom-call(bf16[16,608,128]{2,1,0:T(8,128)(2,1)} %all-to-all-done.3.refs_0_, bf16[1024,3072]{1,0:T(8,128)(2,1)} %refs_3_.5, bf16[1024,3072]{1,0:T(8,128)(2,1)} %refs_3_.5, bf16[1024,3072]{1,0:T(8,128)(2,1)} %refs_3_.5, bf16[392,1024]{1,0:T(8,128)(2,1)} %bitcast.240, f32[1,1024]{1,0:T(1,128)} %bitcast.235, ...), custom_call_target="tpu_custom_call" | custom-call | flops 11500000256 | bytes 1048576 | tf_op jit(solution)/shard_map/finish/pallas_call | solution.py:762
  422.3 1.3 bitcast_add_fusion.9
  423.9 1.1 copy.143
  426.5 1.9 bitcast_add_fusion.6
  431.0 1.2 fusion.11
  432.2 1.3 dynamic-slice_divide_fusion
  (159 shorter events, 25.1 us)
Async XLA Ops:
  21.0 7.6 %copy-start.19 = (s32[1,3,392]{2,0,1:T(1,128)S(1)}, s32[1,3,392]{2,0,1:T(1,128)}, u32[]{:S(2)}) copy-start(s32[1,3,392]{2,0,1:T(1,128)} %param.69) | copy-start | bytes 14116
  21.0 7.6 %copy-start.13 = (bf16[392,1024]{1,0:T(8,128)(2,1)S(1)}, bf16[392,1024]{1,0:T(8,128)(2,1)}, u32[]{:S(2)}) copy-start(bf16[392,1024]{1,0:T(8,128)(2,1)} %get-tuple-element.281) | copy-start | bytes 2408452
  21.0 55.5 %all-to-all-start = ((bf16[16,608,128]{2,1,0:T(8,128)(2,1)}), bf16[16,608,128]{2,1,0:T(8,128)(2,1)S(1)}, u32[]{:S(2)}, u32[]{:S(2)}) async-start(bf16[16,608,128]{2,1,0:T(8,128)(2,1)} %get-tuple-element.274), calls=%async_computation | async-start | bytes 4980736 | tf_op jit(solution)/shard_map/all_to_all | solution.py:875
  28.6 194.6 %all-gather.3.cloned.1.call-start = ((), (), s32[]{:S(2)}) async-start(), calls=%async_computation.5 | async-start | bytes 13926400 | tf_op jit(solution)/shard_map/all_gather | solution.py:886
  76.5 1.5 copy-start.8
  107.2 46.4 %all-to-all-start.1 = ((bf16[16,208,128]{2,1,0:T(8,128)(2,1)}), bf16[16,208,128]{2,1,0:T(8,128)(2,1)S(1)}, u32[]{:S(2)}, u32[]{:S(2)}) async-start(bf16[16,208,128]{2,1,0:T(8,128)(2,1)} %get-tuple-element.275), calls=%async_computation.1 | async-start | bytes 1703936 | tf_op jit(solution)/shard_map/all_to_all | solution.py:892
  153.5 0.9 copy-start.11
  182.5 6.2 %copy-start.20 = (f32[1,1024]{1,0:T(1,128)S(1)}, f32[1,1024]{1,0:T(1,128)}, u32[]{:S(2)}) copy-start(f32[1,1024]{1,0:T(1,128)} %get-tuple-element.301) | copy-start | bytes 12292
  182.5 13.6 %collective-permute-start = (bf16[392,9216]{1,0:T(8,128)(2,1)}, bf16[392,9216]{1,0:T(8,128)(2,1)}, u32[]{:S(2)}, u32[]{:S(2)}) collective-permute-start(bf16[392,9216]{1,0:T(8,128)(2,1)} %get-tuple-element.279.refs_5_.refs_7_.refs_9_.refs_11_), channel_id=1, source_target_pairs={{0,2},{2,0},{4,6},{6,4},{8,10},{10,8},{12,14},{14,12},{16,18},{18,... | collective-permute-start | bytes 21676040 | tf_op jit(solution)/shard_map/ppermute | solution.py:870
  182.6 13.5 %collective-permute-start.1 = (bf16[392,1024]{1,0:T(8,128)(2,1)}, bf16[392,1024]{1,0:T(8,128)(2,1)}, u32[]{:S(2)}, u32[]{:S(2)}) collective-permute-start(bf16[392,1024]{1,0:T(8,128)(2,1)} %bitcast.215), channel_id=1, source_target_pairs={{0,2},{2,0},{4,6},{6,4},{8,10},{10,8},{12,14},{14,12},{16,18},{18,... | collective-permute-start | bytes 2408456 | tf_op jit(solution)/shard_map/ppermute | solution.py:870
  188.7 1.7 copy-start.22
  190.3 3.9 collective-permute-start.5
  190.5 40.6 %all-to-all-start.2 = ((bf16[16,208,128]{2,1,0:T(8,128)(2,1)}), bf16[16,208,128]{2,1,0:T(8,128)(2,1)S(1)}, u32[]{:S(2)}, u32[]{:S(2)}) async-start(bf16[16,208,128]{2,1,0:T(8,128)(2,1)} %get-tuple-element.277), calls=%async_computation.2 | async-start | bytes 1703936 | tf_op jit(solution)/shard_map/all_to_all | solution.py:875
  194.2 81.3 %collective-permute-start.6 = (bf16[2,2,2,256]{3,2,1,0:T(2,128)(2,1)S(1)}, bf16[2,2,2,256]{3,2,1,0:T(2,128)(2,1)S(1)}, u32[]{:S(2)}, u32[]{:S(2)}) collective-permute-start(bf16[2,2,2,256]{3,2,1,0:T(2,128)(2,1)S(1)} %fusion.32), channel_id=1, source_target_pairs={{0,8},{2,10},{4,12},{6,14},{8,0},{10,2},{12,4},{14,6},{16,24},{18,... | collective-permute-start | bytes 12296 | tf_op jit(solution)/shard_map/ppermute | solution.py:821
  215.3 5.0 %copy-start.15 = (bf16[2,128,1024]{2,1,0:T(8,128)(2,1)S(1)}, bf16[2,128,1024]{2,1,0:T(8,128)(2,1)}, u32[]{:S(2)}) copy-start(bf16[2,128,1024]{2,1,0:T(8,128)(2,1)} %get-tuple-element.295) | copy-start | bytes 1572868
  215.3 6.4 %copy-start.9 = (bf16[4,256,1024]{2,1,0:T(8,128)(2,1)S(1)}, bf16[4,256,1024]{2,1,0:T(8,128)(2,1)}, u32[]{:S(2)}) copy-start(bf16[4,256,1024]{2,1,0:T(8,128)(2,1)} %get-tuple-element.288) | copy-start | bytes 6291460
  218.6 57.0 %collective-permute-start.2 = (bf16[2,2,2,128,1024]{4,3,0,1,2:T(8,128)(2,1)}, bf16[2,2,2,128,1024]{4,3,0,1,2:T(8,128)(2,1)}, u32[]{:S(2)}, u32[]{:S(2)}) collective-permute-start(bf16[2,2,2,128,1024]{4,3,0,1,2:T(8,128)(2,1)} %copy.121), channel_id=1, source_target_pairs={{0,4},{2,6},{4,0},{6,2},{8,12},{10,14},{12,8},{14,10},{16,20},{18,... | collective-permute-start | bytes 6291464 | tf_op jit(solution)/shard_map/ppermute | solution.py:821
  220.0 55.5 %collective-permute-start.3 = (bf16[2,2,2,128,1024]{4,3,2,1,0:T(8,128)(2,1)}, bf16[2,2,2,128,1024]{4,3,2,1,0:T(8,128)(2,1)}, u32[]{:S(2)}, u32[]{:S(2)}) collective-permute-start(bf16[2,2,2,128,1024]{4,3,2,1,0:T(8,128)(2,1)} %bitcast.237), channel_id=1, source_target_pairs={{0,1},{1,0},{2,3},{3,2},{4,5},{5,4},{6,7},{7,6},{8,9},{9,8},{10,11... | collective-permute-start | bytes 6291464 | tf_op jit(solution)/shard_map/ppermute | solution.py:817
  221.1 54.5 %collective-permute-start.4 = (bf16[2,2,2,32,1024]{4,3,0,1,2:T(8,128)(2,1)}, bf16[2,2,2,32,1024]{4,3,0,1,2:T(8,128)(2,1)}, u32[]{:S(2)}, u32[]{:S(2)}) collective-permute-start(bf16[2,2,2,32,1024]{4,3,0,1,2:T(8,128)(2,1)} %copy.122), channel_id=1, source_target_pairs={{0,8},{2,10},{4,12},{6,14},{8,0},{10,2},{12,4},{14,6},{16,24},{18,... | collective-permute-start | bytes 1572872 | tf_op jit(solution)/shard_map/ppermute | solution.py:821
  231.1 0.9 copy-start.12
  275.6 2.8 copy-start.4
  275.6 2.8 copy-start.5
  277.3 1.1 copy-start.6
  278.4 4.3 copy-start.10
  282.7 32.6 %collective-permute-start.7 = (bf16[2,2,128,1024]{3,2,0,1:T(8,128)(2,1)}, bf16[2,2,128,1024]{3,2,0,1:T(8,128)(2,1)}, u32[]{:S(2)}, u32[]{:S(2)}) collective-permute-start(bf16[2,2,128,1024]{3,2,0,1:T(8,128)(2,1)} %get-tuple-element.333), channel_id=1, source_target_pairs={{0,1},{1,0},{2,3},{3,2},{4,5},{5,4},{6,7},{7,6},{8,9},{9,8},{10,11... | collective-permute-start | bytes 3145736 | tf_op jit(solution)/shard_map/ppermute | solution.py:817
  286.9 28.5 %collective-permute-start.8 = (bf16[2,2,128,1024]{3,2,1,0:T(8,128)(2,1)}, bf16[2,2,128,1024]{3,2,1,0:T(8,128)(2,1)}, u32[]{:S(2)}, u32[]{:S(2)}) collective-permute-start(bf16[2,2,128,1024]{3,2,1,0:T(8,128)(2,1)} %get-tuple-element.327), channel_id=1, source_target_pairs={{0,4},{2,6},{4,0},{6,2},{8,12},{10,14},{12,8},{14,10},{16,20},{18,... | collective-permute-start | bytes 3145736 | tf_op jit(solution)/shard_map/ppermute | solution.py:821
  287.1 28.2 %collective-permute-start.9 = (bf16[2,2,40,1024]{3,2,0,1:T(8,128)(2,1)S(1)}, bf16[2,2,40,1024]{3,2,0,1:T(8,128)(2,1)S(1)}, u32[]{:S(2)}, u32[]{:S(2)}) collective-permute-start(bf16[2,2,40,1024]{3,2,0,1:T(8,128)(2,1)S(1)} %fusion.12), channel_id=1, source_target_pairs={{0,1},{1,0},{2,3},{3,2},{4,5},{5,4},{6,7},{7,6},{8,9},{9,8},{10,11... | collective-permute-start | bytes 983048 | tf_op jit(solution)/shard_map/ppermute | solution.py:817
  315.3 0.7 copy-start.16
  316.1 3.4 copy-start
  319.4 2.8 copy-start.7
  319.4 2.8 copy-start.17
  323.0 83.2 %all-to-all-start.3 = ((bf16[16,608,128]{2,1,0:T(8,128)(2,1)}), bf16[16,608,128]{2,1,0:T(8,128)(2,1)}, u32[]{:S(2)}, u32[]{:S(2)}) async-start(bf16[16,608,128]{2,1,0:T(8,128)(2,1)} %attend_back_last.1.refs_0_), calls=%async_computation.3 | async-start | bytes 4980736 | tf_op jit(solution)/shard_map/all_to_all | solution.py:976
  329.0 54.9 %collective-permute-start.13 = (bf16[2,128,1024]{2,1,0:T(8,128)(2,1)}, bf16[2,128,1024]{2,1,0:T(8,128)(2,1)}, u32[]{:S(2)}, u32[]{:S(2)}) collective-permute-start(bf16[2,128,1024]{2,1,0:T(8,128)(2,1)} %get-tuple-element.331), channel_id=1, source_target_pairs={{0,8},{2,10},{4,12},{6,14},{8,0},{10,2},{12,4},{14,6},{16,24},{18,... | collective-permute-start | bytes 1572872 | tf_op jit(solution)/shard_map/ppermute | solution.py:821
  330.9 71.2 %collective-permute-start.15 = (bf16[2,128,1024]{2,1,0:T(8,128)(2,1)S(1)}, bf16[2,128,1024]{2,1,0:T(8,128)(2,1)}, u32[]{:S(2)}, u32[]{:S(2)}) collective-permute-start(bf16[2,128,1024]{2,1,0:T(8,128)(2,1)S(1)} %get-tuple-element.329), channel_id=1, source_target_pairs={{0,8},{2,10},{4,12},{6,14},{8,0},{10,2},{12,4},{14,6},{16,24},{18,... | collective-permute-start | bytes 1572872 | tf_op jit(solution)/shard_map/ppermute | solution.py:821
  343.2 58.9 %copy-start.1 = (f32[2,1,128,1024]{3,2,0,1:T(8,128)S(1)}, f32[2,1,128,1024]{3,2,0,1:T(8,128)}, u32[]{:S(2)}) copy-start(f32[2,1,128,1024]{3,2,0,1:T(8,128)} %get-tuple-element.328) | copy-start | bytes 3145732
  343.2 61.1 %copy-start.3 = (f32[1024,256]{1,0:T(8,128)S(1)}, f32[1024,256]{1,0:T(8,128)}, u32[]{:S(2)}) copy-start(f32[1024,256]{1,0:T(8,128)} %triple_grad.1) | copy-start | bytes 3145732
  345.2 59.0 %collective-permute-start.10 = (f32[16,32,256]{2,1,0:T(8,128)}, f32[16,32,256]{2,1,0:T(8,128)}, u32[]{:S(2)}, u32[]{:S(2)}) collective-permute-start(f32[16,32,256]{2,1,0:T(8,128)} %dynamic-slice_bitcast_fusion), channel_id=1, source_target_pairs={{0,1},{1,0},{2,3},{3,2},{4,5},{5,4},{6,7},{7,6},{8,9},{9,8},{10,11... | collective-permute-start | bytes 1572872 | tf_op jit(solution)/shard_map/ppermute | solution.py:995
  345.5 10.1 %collective-permute-start.11 = (bf16[2,40,1024]{2,1,0:T(8,128)(2,1)}, bf16[2,40,1024]{2,1,0:T(8,128)(2,1)S(1)}, u32[]{:S(2)}, u32[]{:S(2)}) collective-permute-start(bf16[2,40,1024]{2,1,0:T(8,128)(2,1)} %get-tuple-element.337), channel_id=1, source_target_pairs={{0,4},{2,6},{4,0},{6,2},{8,12},{10,14},{12,8},{14,10},{16,20},{18,... | collective-permute-start | bytes 491528 | tf_op jit(solution)/shard_map/ppermute | solution.py:821
  355.7 50.6 %copy-start.18 = (bf16[2,40,1024]{2,1,0:T(8,128)(2,1)}, bf16[2,40,1024]{2,1,0:T(8,128)(2,1)S(1)}, u32[]{:S(2)}) copy-start(bf16[2,40,1024]{2,1,0:T(8,128)(2,1)S(1)} %collective-permute-done.11) | copy-start | bytes 491524
  355.7 64.8 %collective-permute-start.12 = (bf16[40,1024]{1,0:T(8,128)(2,1)S(1)}, bf16[40,1024]{1,0:T(8,128)(2,1)}, u32[]{:S(2)}, u32[]{:S(2)}) collective-permute-start(bf16[40,1024]{1,0:T(8,128)(2,1)S(1)} %fusion.18), channel_id=1, source_target_pairs={{0,16},{2,18},{4,20},{6,22},{8,24},{10,26},{12,28},{14,30},{16,0},... | collective-permute-start | bytes 245768 | tf_op jit(solution)/shard_map/ppermute | solution.py:821
  385.8 36.4 %collective-permute-start.14 = (bf16[128,1024]{1,0:T(8,128)(2,1)}, bf16[128,1024]{1,0:T(8,128)(2,1)}, u32[]{:S(2)}, u32[]{:S(2)}) collective-permute-start(bf16[128,1024]{1,0:T(8,128)(2,1)} %fusion.14), channel_id=1, source_target_pairs={{0,16},{2,18},{4,20},{6,22},{8,24},{10,26},{12,28},{14,30},{16,0},... | collective-permute-start | bytes 786440 | tf_op jit(solution)/shard_map/ppermute | solution.py:821
  403.8 21.9 %collective-permute-start.16 = (bf16[128,1024]{1,0:T(8,128)(2,1)}, bf16[128,1024]{1,0:T(8,128)(2,1)}, u32[]{:S(2)}, u32[]{:S(2)}) collective-permute-start(bf16[128,1024]{1,0:T(8,128)(2,1)} %fusion.15), channel_id=1, source_target_pairs={{0,16},{2,18},{4,20},{6,22},{8,24},{10,26},{12,28},{14,30},{16,0},... | collective-permute-start | bytes 786440 | tf_op jit(solution)/shard_map/ppermute | solution.py:821
  406.2 22.1 %all-to-all-start.4 = ((f32[16,32,256]{2,1,0:T(8,128)}), f32[16,32,256]{2,1,0:T(8,128)S(1)}, u32[]{:S(2)}, u32[]{:S(2)}) async-start(f32[16,32,256]{2,1,0:T(8,128)} %bitcast_add_fusion.4), calls=%async_computation.4 | async-start | bytes 1048576 | tf_op jit(solution)/shard_map/all_to_all | solution.py:996
  421.5 5.0 %copy-start.2 = (f32[2,1,128,1024]{3,2,0,1:T(8,128)S(1)}, f32[2,1,128,1024]{3,2,0,1:T(8,128)}, u32[]{:S(2)}) copy-start(f32[2,1,128,1024]{3,2,0,1:T(8,128)} %get-tuple-element.328) | copy-start | bytes 3145732
  431.0 2.6 copy-start.14
  432.2 1.3 copy-start.21
Sparse Core Ops, SparseCore 0:
  76.7 94.2 all-gather.2
